TPU v7x, 256 devices: a whole 4x4x8 slice. The times are simulated.
256 devices in a mesh: grp: 8 (over y, core), cache: 32 (over x, z).
Axes of the slice: x: 4, y: 4, z: 8, core: 2. Of those that a mesh axis runs over, the one named last changes fastest.
Arguments:
- queries: bfloat16 [2048, 4, 8192], P(('grp', 'cache')), may hold values from -6 to 6
- new_kv: bfloat16 [2048, 4, 2048], P(('grp', 'cache')), may hold values from -6 to 6
- kv_cache: bfloat16 [4096, 128, 2048], P(('grp', 'cache')), may hold values from -6 to 6
- page_owner: int32 [2048, 4], P(('grp', 'cache')), may hold values from 0 to 31, all different within a row; in each aligned block of 8 rows (0 to 7, 8 to 15, ...) at most 2 rows name the same one
- page_index: int32 [2048, 4, 1], P(('grp', 'cache')), may hold values from 0 to 15
- lengths: int32 [2048], P(('grp', 'cache')), may hold values from 1 to 512, as said below
Outputs:
- attention_out: bfloat16 [2048, 4, 8192], P(('grp', 'cache'))
Inputs may be any that keep to these rules, and one draw needn't show every extreme that they name: `page_owner`: each row names 4 different owners; among the 8 rows held by one device no owner is named by more than 2 rows, and in every draw some owner is named by exactly 2 rows of some device. `lengths`: some request has exactly 512 valid tokens in every draw.
All inputs are finite; a program needn't handle non-finite values.
Results may differ from a plain program's by a relative error of at most 0.0051.
Values may be sent and summed in bfloat16 or wider, within the bound.
A program may use at most 192 MiB of HBM per device.

v0:
```python
from functools import partial
import math

import jax
import jax.numpy as jnp
from jax import lax
from jax.sharding import PartitionSpec as P

KVH = 8
HD = 128
GQ = 8
STEPS = 4
PAGE = 128
SEL = 4
PPO = 1


neg_fill = -1e30
block_rows = 16


def item_partial(query_row, panel_rows, valid_count):
    token_count = panel_rows.shape[0]
    query_heads = query_row.reshape(STEPS, KVH, GQ, HD)
    key_rows = panel_rows[:, : KVH * HD].reshape(token_count, KVH, HD)
    value_rows = panel_rows[:, KVH * HD :].reshape(token_count, KVH, HD)
    scores = jnp.einsum(
        "tkgd,ukd->tkgu", query_heads, key_rows, preferred_element_type=jnp.float32
    ) * (1.0 / math.sqrt(HD))
    usable = jnp.arange(token_count, dtype=jnp.int32) < valid_count
    scores = jnp.where(usable, scores, neg_fill)
    highest = jnp.max(scores, axis=-1)
    weights = jnp.where(usable, jnp.exp(scores - highest[..., None]), 0.0)
    weight_sum = jnp.sum(weights, axis=-1)
    mixture = jnp.einsum(
        "tkgu,ukd->tkgd",
        weights.astype(jnp.bfloat16),
        value_rows,
        preferred_element_type=jnp.float32,
    )
    normed = (mixture / jnp.maximum(weight_sum, 1.0)[..., None]).astype(jnp.bfloat16)
    return (
        normed.reshape(STEPS, KVH * GQ * HD),
        highest.reshape(STEPS, KVH * GQ),
        weight_sum.reshape(STEPS, KVH * GQ),
    )


def new_partial(query_row, new_row):
    query_heads = query_row.reshape(STEPS, KVH, GQ, HD)
    key_rows = new_row[:, : KVH * HD].reshape(STEPS, KVH, HD)
    value_rows = new_row[:, KVH * HD :].reshape(STEPS, KVH, HD)
    scores = jnp.einsum(
        "tkgd,ukd->tkgu", query_heads, key_rows, preferred_element_type=jnp.float32
    ) * (1.0 / math.sqrt(HD))
    causal = (jnp.arange(STEPS)[:, None] >= jnp.arange(STEPS)[None, :])[:, None, None, :]
    scores = jnp.where(causal, scores, neg_fill)
    highest = jnp.max(scores, axis=-1)
    weights = jnp.where(causal, jnp.exp(scores - highest[..., None]), 0.0)
    weight_sum = jnp.sum(weights, axis=-1)
    mixture = jnp.einsum(
        "tkgu,ukd->tkgd",
        weights.astype(jnp.bfloat16),
        value_rows,
        preferred_element_type=jnp.float32,
    )
    return (
        mixture.reshape(STEPS, KVH * GQ, HD),
        highest.reshape(STEPS, KVH * GQ),
        weight_sum.reshape(STEPS, KVH * GQ),
    )


def plan_slots(owner_table, page_table, length_rows, owner_ids, capacity):
    visitor_count = owner_table.shape[0]
    matches = (owner_table[:, :, None] == owner_ids[None, None, :]).astype(jnp.int32)
    hit_table = jnp.sum(matches, axis=1)
    slot_rank = jnp.cumsum(hit_table, axis=0) - hit_table
    slot_ids = jnp.arange(capacity, dtype=jnp.int32)
    select = hit_table.T[:, None, :] * (slot_rank.T[:, None, :] == slot_ids[None, :, None]).astype(
        jnp.int32
    )
    item_span = PPO * PAGE
    starts = jnp.arange(SEL, dtype=jnp.int32) * item_span
    counts = jnp.clip(length_rows[:, None] - starts[None, :], 0, item_span)
    item_count = jnp.sum(matches * counts[:, :, None], axis=1)
    item_pages = jnp.sum(matches[:, :, :, None] * page_table[:, :, None, :], axis=1)
    item_meta = jnp.concatenate([item_count[:, :, None], item_pages], axis=2)
    slot_meta = jnp.sum(
        select[:, :, :, None] * jnp.transpose(item_meta, (1, 0, 2))[:, None, :, :], axis=2
    )
    slot_visitor = jnp.sum(
        select * jnp.arange(visitor_count, dtype=jnp.int32)[None, None, :], axis=2
    )
    return (select, slot_meta, hit_table, slot_rank, slot_visitor)


def owner_work(item_queries, item_meta, kv_cache):
    first_dim = item_queries.shape[0]
    second_dim = item_queries.shape[1]
    row_count = first_dim * second_dim
    flat_queries = item_queries.reshape(row_count, STEPS, -1)
    flat_meta = item_meta.reshape(row_count, -1)
    pieces_out = []
    pieces_top = []
    pieces_sum = []
    for offset in range(0, row_count, block_rows):
        finish = min(offset + block_rows, row_count)
        meta_part = flat_meta[offset:finish]
        panel_rows = kv_cache[meta_part[:, 1:]].reshape(finish - offset, -1, kv_cache.shape[2])
        part_out, part_top, part_sum = jax.vmap(item_partial)(
            flat_queries[offset:finish], panel_rows, meta_part[:, 0]
        )
        pieces_out.append(part_out)
        pieces_top.append(part_top)
        pieces_sum.append(part_sum)
    whole_out = jnp.concatenate(pieces_out, axis=0).reshape(first_dim, second_dim, -1)
    whole_top = jnp.concatenate(pieces_top, axis=0).reshape(first_dim, second_dim, -1)
    whole_sum = jnp.concatenate(pieces_sum, axis=0).reshape(first_dim, second_dim, -1)
    return (whole_out, whole_top, whole_sum)


def per_device(queries, new_kv, kv_cache, page_owner, page_index, lengths):
    group_count = lax.axis_size("grp")
    owner_count = lax.axis_size("cache")
    visitor_count = queries.shape[0]
    per_group = visitor_count // group_count
    capacity = max(2, (2 * visitor_count * SEL + owner_count - 1) // owner_count)
    sent_queries = queries.reshape(group_count, per_group, STEPS, -1)
    sent_new = new_kv.reshape(group_count, per_group, STEPS, -1)
    got_queries, got_new = (
        lax.all_to_all(sent_queries, "grp", split_axis=0, concat_axis=0, tiled=True),
        lax.all_to_all(sent_new, "grp", split_axis=0, concat_axis=0, tiled=True),
    )
    visit_queries = got_queries.reshape(visitor_count, STEPS, -1)
    visit_new = got_new.reshape(visitor_count, STEPS, -1)
    owner_ids = jnp.arange(owner_count, dtype=jnp.int32)
    select, slot_meta, hit_table, slot_rank, slot_visitor = plan_slots(
        page_owner, page_index, lengths, owner_ids, capacity
    )
    flat_queries = visit_queries.reshape(visitor_count, -1)
    all_queries, all_owner, all_pages, all_len = (
        lax.all_gather(flat_queries, "cache", axis=0, tiled=True),
        lax.all_gather(page_owner, "cache", axis=0, tiled=True),
        lax.all_gather(page_index, "cache", axis=0, tiled=True),
        lax.all_gather(lengths, "cache", axis=0, tiled=True),
    )
    owner_here = lax.axis_index("cache")
    owner_list = jnp.reshape(owner_here, (1,))
    plan_each = jax.vmap(partial(plan_slots, capacity=capacity), in_axes=(0, 0, 0, None))
    select_all, meta_all, unused_hits, unused_rank, unused_visitor = plan_each(
        all_owner.reshape(owner_count, visitor_count, SEL),
        all_pages.reshape(owner_count, visitor_count, SEL, PPO),
        all_len.reshape(owner_count, visitor_count),
        owner_list,
    )
    select_here = select_all[:, 0]
    meta_here = meta_all[:, 0]
    slot_queries = jnp.einsum(
        "scr,srx->scx",
        select_here.astype(jnp.bfloat16),
        all_queries.reshape(owner_count, visitor_count, -1),
        preferred_element_type=jnp.float32,
    ).astype(jnp.bfloat16)
    part_out, part_top, part_sum = owner_work(slot_queries, meta_here, kv_cache)
    back_out = lax.all_to_all(part_out, "cache", split_axis=0, concat_axis=0, tiled=True)
    back_top, back_sum = (
        lax.all_to_all(part_top, "cache", split_axis=0, concat_axis=0, tiled=True),
        lax.all_to_all(part_sum, "cache", split_axis=0, concat_axis=0, tiled=True),
    )
    new_mix, new_top, new_sum = jax.vmap(new_partial)(visit_queries, visit_new)
    head_rows = STEPS * KVH * GQ
    new_top_flat = new_top.reshape(visitor_count, head_rows)
    new_sum_flat = new_sum.reshape(visitor_count, head_rows)
    slot_index = jnp.clip(slot_rank, 0, capacity - 1).T
    item_top = jnp.take_along_axis(back_top, slot_index[:, :, None], axis=1)
    item_sum = jnp.take_along_axis(back_sum, slot_index[:, :, None], axis=1)
    present = hit_table.T[:, :, None] > 0
    item_top = jnp.where(present, item_top, neg_fill)
    item_sum = jnp.where(present, item_sum, 0.0)
    peak_score = jnp.maximum(new_top_flat, jnp.max(item_top, axis=0))
    item_weight = jnp.exp(item_top - peak_score[None]) * item_sum
    new_weight = jnp.exp(new_top_flat - peak_score)
    denominator = jnp.sum(item_weight, axis=0) + new_weight * new_sum_flat
    slot_peak = peak_score[slot_visitor]
    slot_weight = jnp.exp(back_top - slot_peak) * back_sum
    back_values = back_out.astype(jnp.float32).reshape(owner_count, capacity, head_rows, HD)
    weighted = (slot_weight[..., None] * back_values).reshape(owner_count, capacity, -1)
    numerator = jnp.einsum(
        "ocr,ocx->rx", select.astype(jnp.float32), weighted, precision=lax.Precision.HIGHEST
    )
    numerator = (
        numerator.reshape(visitor_count, STEPS, KVH * GQ, HD)
        + new_weight.reshape(visitor_count, STEPS, KVH * GQ, 1) * new_mix
    )
    result_rows = (numerator / denominator.reshape(visitor_count, STEPS, KVH * GQ, 1)).astype(
        jnp.bfloat16
    )
    result_rows = result_rows.reshape(group_count, per_group, STEPS, -1)
    at_home = lax.all_to_all(result_rows, "grp", split_axis=0, concat_axis=0, tiled=True)
    return at_home.reshape(visitor_count, STEPS, -1)


def solution(mesh):
    in_specs = (
        P(("grp", "cache"), None, None),
        P(("grp", "cache"), None, None),
        P(("grp", "cache"), None, None),
        P(("grp", "cache"), None),
        P(("grp", "cache"), None, None),
        P(("grp", "cache")),
    )
    out_specs = P(("grp", "cache"), None, None)
    return jax.shard_map(
        per_device, mesh=mesh, in_specs=in_specs, out_specs=out_specs, check_vma=False
    )
```

profile of v0, /device:TPU:1, one launch (start us, length us, event | category | flops | bytes accessed | tf_op | source)
XLA Modules:
  0.0 512.8 jit_solution(2753819225060617268)
XLA Ops:
  6.6 16.1 %all_to_all.30 = bf16[8,1,4,8192]{3,2,1,0:T(4,128)(2,1)S(1)} all-to-all(bf16[8,1,4,8192]{3,2,1,0:T(4,128)(2,1)} %bitcast.300), channel_id=1, replica_groups=mesh['grp'=8,'cache'=32] {'grp'}, dimensions={0} | all-to-all | bytes 1048576 | tf_op jit(solution)/shard_map/all_to_all | solution.py:132
  22.7 1.1 copy.421
  23.8 4.9 all-to-all-start.2
  28.8 42.9 %all-gather = s32[32,8,4]{1,2,0:T(4,128)S(1)} all-gather(s32[1,8,4]{1,2,0:T(4,128)S(1)} %bitcast.305), channel_id=1, replica_groups=mesh['grp'=8,'cache'=32] {'cache'}, dimensions={0}, use_global_device_ids=true | all-gather | bytes 4224 | tf_op jit(solution)/shard_map/all_gather | solution.py:144
  73.5 13.8 %all-reduce = s32[256]{0:T(256)S(1)} all-reduce(s32[256]{0:T(256)S(1)} %dynamic-update-slice), channel_id=1, replica_groups=mesh['grp'=8,'cache'=32] {'cache'}, use_global_device_ids=true, to_apply=%add | all-reduce | flops 256 | bytes 2048
  88.1 37.2 %all_gather.14 = s32[256,4,1]{1,2,0:T(1,128)S(1)} all-gather(s32[8,4,1]{1,2,0:T(1,128)S(1)} %copy.326), channel_id=1, replica_groups=mesh['grp'=8,'cache'=32] {'cache'}, dimensions={0}, use_global_device_ids=true | all-gather | bytes 4224 | tf_op jit(solution)/shard_map/all_gather | solution.py:145
  126.4 8.6 %gather_fusion.1 = bf16[16,128,2048]{2,1,0:T(8,128)(2,1)} fusion(bf16[16,128,2048]{2,1,0:T(8,128)(2,1)} %param.10, s32[1024]{0:T(1024)S(1)} %pad_clamp_fusion.3), kind=kCustom, calls=%fused_computation.3 | custom fusion | bytes 16777280 | tf_op jit(solution)/shard_map/gather | solution.py:110
  135.0 6.2 %fusion.117 = (bf16[16,128,1024]{2,1,0:T(8,128)(2,1)}, bf16[16,128,1024]{2,1,0:T(8,128)(2,1)}) fusion(bf16[16,128,2048]{2,1,0:T(8,128)(2,1)} %gather_fusion.1), kind=kLoop, calls=%fused_computation.179 | loop fusion | bytes 16777216 | tf_op jit(solution)/shard_map/vmap()/slice | solution.py:26
  141.2 6.4 %copy.367 = bf16[16,128,1024]{1,2,0:T(8,128)(2,1)} copy(bf16[16,128,1024]{2,1,0:T(8,128)(2,1)} %get-tuple-element.14) | data formatting | bytes 8388608 | tf_op jit(solution)/shard_map/vmap()/slice | solution.py:26
  147.6 6.4 %copy.337 = bf16[16,128,1024]{1,2,0:T(8,128)(2,1)} copy(bf16[16,128,1024]{2,1,0:T(8,128)(2,1)} %get-tuple-element.15) | data formatting | bytes 8388608 | tf_op jit(solution)/shard_map/vmap()/slice | solution.py:25
  154.0 8.1 %gather_fusion.2 = bf16[16,128,2048]{2,1,0:T(8,128)(2,1)} fusion(bf16[16,128,2048]{2,1,0:T(8,128)(2,1)} %param.10, s32[1024]{0:T(1024)S(1)} %pad_clamp_fusion.2), kind=kCustom, calls=%fused_computation.4 | custom fusion | bytes 16777280 | tf_op jit(solution)/shard_map/gather | solution.py:110
  162.1 6.1 %fusion.118 = (bf16[16,128,1024]{2,1,0:T(8,128)(2,1)}, bf16[16,128,1024]{2,1,0:T(8,128)(2,1)}) fusion(bf16[16,128,2048]{2,1,0:T(8,128)(2,1)} %gather_fusion.2), kind=kLoop, calls=%fused_computation.180 | loop fusion | bytes 16777216 | tf_op jit(solution)/shard_map/vmap()/slice | solution.py:26
  168.2 6.4 %copy.370 = bf16[16,128,1024]{1,2,0:T(8,128)(2,1)} copy(bf16[16,128,1024]{2,1,0:T(8,128)(2,1)} %get-tuple-element.16) | data formatting | bytes 8388608 | tf_op jit(solution)/shard_map/vmap()/slice | solution.py:26
  174.6 6.4 %copy.342 = bf16[16,128,1024]{1,2,0:T(8,128)(2,1)} copy(bf16[16,128,1024]{2,1,0:T(8,128)(2,1)} %get-tuple-element.17) | data formatting | bytes 8388608 | tf_op jit(solution)/shard_map/vmap()/slice | solution.py:25
  181.0 8.0 %gather_fusion.3 = bf16[16,128,2048]{2,1,0:T(8,128)(2,1)} fusion(bf16[16,128,2048]{2,1,0:T(8,128)(2,1)} %param.10, s32[1024]{0:T(1024)S(1)} %pad_clamp_fusion.1), kind=kCustom, calls=%fused_computation.5 | custom fusion | bytes 16777280 | tf_op jit(solution)/shard_map/gather | solution.py:110
  189.0 6.1 %fusion.119 = (bf16[16,128,1024]{2,1,0:T(8,128)(2,1)}, bf16[16,128,1024]{2,1,0:T(8,128)(2,1)}) fusion(bf16[16,128,2048]{2,1,0:T(8,128)(2,1)} %gather_fusion.3), kind=kLoop, calls=%fused_computation.181 | loop fusion | bytes 16777216 | tf_op jit(solution)/shard_map/vmap()/slice | solution.py:26
  195.1 6.4 %copy.373 = bf16[16,128,1024]{1,2,0:T(8,128)(2,1)} copy(bf16[16,128,1024]{2,1,0:T(8,128)(2,1)} %get-tuple-element.18) | data formatting | bytes 8388608 | tf_op jit(solution)/shard_map/vmap()/slice | solution.py:26
  201.5 6.4 %copy.347 = bf16[16,128,1024]{1,2,0:T(8,128)(2,1)} copy(bf16[16,128,1024]{2,1,0:T(8,128)(2,1)} %get-tuple-element.19) | data formatting | bytes 8388608 | tf_op jit(solution)/shard_map/vmap()/slice | solution.py:25
  207.9 8.0 %gather_fusion = bf16[16,128,2048]{2,1,0:T(8,128)(2,1)} fusion(bf16[16,128,2048]{2,1,0:T(8,128)(2,1)} %param.10, s32[1024]{0:T(1024)S(1)} %pad_clamp_fusion.4), kind=kCustom, calls=%fused_computation.2 | custom fusion | bytes 16777280 | tf_op jit(solution)/shard_map/gather | solution.py:110
  215.9 6.1 %fusion.116 = (bf16[16,128,1024]{2,1,0:T(8,128)(2,1)}, bf16[16,128,1024]{2,1,0:T(8,128)(2,1)}) fusion(bf16[16,128,2048]{2,1,0:T(8,128)(2,1)} %gather_fusion), kind=kLoop, calls=%fused_computation.178 | loop fusion | bytes 16777216 | tf_op jit(solution)/shard_map/vmap()/slice | solution.py:26
  221.9 6.4 %copy.364 = bf16[16,128,1024]{1,2,0:T(8,128)(2,1)} copy(bf16[16,128,1024]{2,1,0:T(8,128)(2,1)} %get-tuple-element.12) | data formatting | bytes 8388608 | tf_op jit(solution)/shard_map/vmap()/slice | solution.py:26
  228.3 6.4 %copy.331 = bf16[16,128,1024]{1,2,0:T(8,128)(2,1)} copy(bf16[16,128,1024]{2,1,0:T(8,128)(2,1)} %get-tuple-element.13) | data formatting | bytes 8388608 | tf_op jit(solution)/shard_map/vmap()/slice | solution.py:25
  235.0 8.4 %convolution_convert_fusion = bf16[32,2,32768]{2,1,0:T(2,128)(2,1)S(1)} fusion(bf16[32,2,8]{2,1,0:T(2,128)(2,1)S(1)} %copy.332, bf16[256,32768]{1,0:T(8,128)(2,1)} %all-gather.3.cloned.1.call-done), kind=kOutput, calls=%fused_computation.7 | convolution fusion | flops 35651584 | bytes 20972544 | tf_op jit(solution)/shard_map/scr,srx->scx/dot_general | solution.py:159
  243.4 4.0 fusion.120
  247.4 2.6 reshape.305
  250.1 2.6 reshape.317
  252.7 1.6 reshape.313
  254.3 2.0 reshape.309
  256.3 3.8 bitcast_reduce_fusion.2
  260.4 1.4 fusion.18
  262.6 4.8 bitcast_reduce_fusion.1
  268.2 2.6 fusion.20
  271.6 3.8 bitcast_reduce_fusion
  276.6 2.4 fusion.22
  279.8 5.5 %bitcast_reduce_fusion.3 = (f32[16,4,8,8]{3,1,2,0:T(4,128)}, f32[16,8,128,4,8]{2,4,3,1,0:T(8,128)}) fusion(pred[16,128]{1,0:T(8,128)(4,1)S(1)} %iota_compare_fusion.5, bf16[16,128,8,128,1]{1,3,4,2,0:T(8,128)(2,1)} %bitcast.289, bf16[16,4,8,8,128]{4,3,2,1,0:T(8,128)(2,1)S(1)} %copy-done.13), kind=kOutput, calls=%fused_computation.34 | convolution fusion | flops 135786496 | bytes 7358464 | tf_op jit(solution)/shard_map/vmap(tkgd,ukd->tkgu)/dot_general | solution.py:27
  285.3 1.2 copy.335
  286.5 2.6 fusion.16
  289.2 5.3 %fusion.5 = bf16[16,4,8,8,128]{4,3,1,2,0:T(8,128)(2,1)S(1)} fusion(bf16[16,128,8,128,1]{1,3,4,2,0:T(8,128)(2,1)} %bitcast.282, f32[16,8,128,4,8]{2,4,3,1,0:T(8,128)} %copy-done.2, f32[16,4,8,8]{3,1,2,0:T(4,128)} %broadcast_maximum_fusion.2, f32[16,4,8,8]{3,1,2,0:T(4,128)S(1)} %copy-done.8, pred[16,128]{1,0:T(8,128)(4,1)S(1)} %iota_compare_fusion.3), kind=kOutput, calls=%fused_computation.18 | convolution fusion | flops 137887744 | bytes 7374848 | tf_op jit(solution)/shard_map/vmap(tkgu,ukd->tkgd)/dot_general | solution.py:35
  294.6 3.5 fusion.4
  298.2 3.3 fusion.3
  302.5 5.5 %all-to-all-start.1 = ((f32[32,2,256]{2,1,0:T(2,128)}), f32[32,2,256]{2,1,0:T(2,128)S(1)}, u32[]{:S(2)}, u32[]{:S(2)}) async-start(f32[32,2,256]{2,1,0:T(2,128)} %reshape.319), calls=%async_computation.1 | async-start | bytes 131072 | tf_op jit(solution)/shard_map/all_to_all | solution.py:168
  308.1 8.0 %fusion.6 = bf16[16,4,8,8,128]{4,3,1,2,0:T(8,128)(2,1)} fusion(bf16[16,128,8,128,1]{1,3,4,2,0:T(8,128)(2,1)} %bitcast.284, f32[16,8,128,4,8]{2,4,3,1,0:T(8,128)} %get-tuple-element.45, f32[16,4,8,8]{3,1,2,0:T(4,128)S(1)} %broadcast_maximum_fusion.3, f32[16,4,8,8]{3,1,2,0:T(4,128)S(1)} %copy-done.6, pred[16,128]{1,0:T(8,128)(4,1)S(1)} %iota_compare_fusion.5), kind=kOutput, calls=%fused_computation.20 | convolution fusion | flops 137887744 | bytes 7374848 | tf_op jit(solution)/shard_map/vmap(tkgu,ukd->tkgd)/dot_general | solution.py:35
  317.7 1.5 copy.372
  319.2 1.3 reshape.334
  320.5 1.5 copy.375
  322.1 1.3 reshape.336
  323.4 1.5 copy.366
  324.9 1.3 reshape.330
  327.2 9.2 %all-to-all-start.3 = ((f32[32,2,256]{2,1,0:T(2,128)}), f32[32,2,256]{2,1,0:T(2,128)S(1)}, u32[]{:S(2)}, u32[]{:S(2)}) async-start(f32[32,2,256]{2,1,0:T(2,128)} %reshape.328), calls=%async_computation.3 | async-start | bytes 131072 | tf_op jit(solution)/shard_map/all_to_all | solution.py:169
  336.4 2.1 pad_maximum_fusion
  338.5 5.2 %copy.376 = bf16[64,4,8192]{2,1,0:T(4,128)(2,1)} copy(bf16[64,4,8192]{2,0,1:T(8,128)(2,1)S(1)} %pad_maximum_fusion) | data formatting | bytes 8388608 | tf_op jit(solution)/shard_map/concatenate | solution.py:117
  343.7 8.4 %reshape.337 = bf16[32,2,32768]{2,1,0:T(2,128)(2,1)} reshape(bf16[64,4,8192]{2,1,0:T(4,128)(2,1)} %copy.376) | data formatting | bytes 8388608 | tf_op jit(solution)/shard_map/reshape | solution.py:117
  352.1 9.7 %all-to-all-start.4 = ((bf16[32,2,32768]{2,1,0:T(2,128)(2,1)}), bf16[32,2,32768]{2,1,0:T(2,128)(2,1)}, u32[]{:S(2)}, u32[]{:S(2)}) async-start(bf16[32,2,32768]{2,1,0:T(2,128)(2,1)} %reshape.337), calls=%async_computation.4 | async-start | bytes 8388608 | tf_op jit(solution)/shard_map/all_to_all | solution.py:166
  363.1 3.3 fusion.122
  367.3 1.3 convolution_bitcast_fusion
  369.2 1.4 gather_fusion.5
  371.6 1.4 gather_fusion.6
  373.5 4.6 mul.141
  378.1 10.5 %mul.142 = f32[32,2,32768]{2,1,0:T(2,128)} reshape(f32[32,2,256,128]{3,2,1,0:T(8,128)} %mul.141) | data formatting | bytes 16777216 | tf_op jit(solution)/shard_map/mul | solution.py:188
  388.6 47.1 %all-to-all-done.4 = bf16[32,2,32768]{2,1,0:T(2,128)(2,1)} async-done(((bf16[32,2,32768]{2,1,0:T(2,128)(2,1)}), bf16[32,2,32768]{2,1,0:T(2,128)(2,1)}, u32[]{:S(2)}, u32[]{:S(2)}) %all-to-all-start.4) | async-done | bytes 4194336 | tf_op jit(solution)/shard_map/all_to_all | solution.py:166
  435.8 9.5 %multiply_bitcast_fusion = f32[32768,2,32]{0,1,2:T(2,128)} fusion(f32[32,2,32768]{2,1,0:T(2,128)} %mul.142, bf16[32,2,32768]{2,1,0:T(2,128)(2,1)} %all-to-all-done.4), kind=kLoop, calls=%fused_computation.11 | loop fusion | flops 4194304 | bytes 20971520 | tf_op jit(solution)/shard_map/ocr,ocx->rx/dot_general | solution.py:189
  445.2 11.8 %reshape.436 = f32[4,64,128,2,32]{2,1,0,3,4:T(8,128)} reshape(f32[32768,2,32]{0,1,2:T(2,128)} %multiply_bitcast_fusion) | data formatting | bytes 16777216 | tf_op jit(solution)/shard_map/ocr,ocx->rx/dot_general | solution.py:189
  457.0 12.6 %fusion.35 = bf16[8,1,4,8192]{3,0,2,1:T(8,128)(2,1)S(1)} fusion(f32[4,64,128,2,32]{2,1,0,3,4:T(8,128)} %reshape.436, f32[8,4,64,128]{3,0,2,1:T(8,128)S(1)} %bitcast.281, f32[8,4,64]{0,2,1:T(8,128)S(1)} %copy.387, f32[8,4,64]{0,2,1:T(8,128)S(1)} %copy.381, s32[32,8]{0,1:T(8,128)S(1)} %bitcast.304, s32[32,8]{0,1:T(8,128)S(1)} %get-tuple-element.11), kind=kOutput, calls=%fused_computation.54 | convolution fusion | flops 202376704 | bytes 9979904 | tf_op jit(solution)/shard_map/ocr,ocx->rx/dot_general | solution.py:189
  470.1 34.8 %all_to_all.31 = bf16[8,1,4,8192]{3,2,1,0:T(4,128)(2,1)S(1)} all-to-all(bf16[8,1,4,8192]{3,2,1,0:T(4,128)(2,1)S(1)} %copy.388), channel_id=1, replica_groups=mesh['grp'=8,'cache'=32] {'grp'}, dimensions={0} | all-to-all | bytes 1048576 | tf_op jit(solution)/shard_map/all_to_all | solution.py:200
  (157 shorter events, 17.0 us)
Async XLA Ops:
  6.5 65.6 %copy-start.23 = (u32[256]{0:T(256)S(1)}, u32[256]{0:T(256)}, u32[]{:S(2)}) copy-start(u32[256]{0:T(256)} %constant.82) | copy-start | bytes 3076
  6.5 22.2 %copy-start.19 = (s32[8,4]{0,1:T(4,128)S(1)}, s32[8,4]{0,1:T(4,128)}, u32[]{:S(2)}) copy-start(s32[8,4]{0,1:T(4,128)} %param.11) | copy-start | bytes 388
  6.5 66.7 %copy-start.22 = (s32[8]{0:T(128)S(1)}, s32[8]{0:T(128)}, u32[]{:S(2)}) copy-start(s32[8]{0:T(128)} %param.13) | copy-start | bytes 100
  6.5 81.1 %copy-start.21 = (s32[8,4,1]{0,2,1:T(1,128)S(1)}, s32[8,4,1]{0,2,1:T(1,128)}, u32[]{:S(2)}) copy-start(s32[8,4,1]{0,2,1:T(1,128)} %param.12) | copy-start | bytes 388
  6.5 228.5 %all-gather.3.cloned.1.call-start = ((), (), s32[]{:S(2)}) async-start(), calls=%async_computation.6 | async-start | bytes 17301504 | tf_op jit(solution)/shard_map/all_gather | solution.py:143
  23.8 278.7 %all-to-all-start.2 = ((bf16[8,1,4,2048]{3,2,1,0:T(4,128)(2,1)}), bf16[8,1,4,2048]{3,2,1,0:T(4,128)(2,1)}, u32[]{:S(2)}, u32[]{:S(2)}) async-start(bf16[8,1,4,2048]{3,2,1,0:T(4,128)(2,1)} %bitcast.33), calls=%async_computation.2 | async-start | bytes 262144 | tf_op jit(solution)/shard_map/all_to_all | solution.py:133
  260.2 7.2 %copy-start.2 = (f32[16,8,128,4,8]{2,4,3,1,0:T(8,128)}, f32[16,8,128,4,8]{2,4,3,1,0:T(8,128)S(1)}, u32[]{:S(2)}) copy-start(f32[16,8,128,4,8]{2,4,3,1,0:T(8,128)S(1)} %get-tuple-element.43) | copy-start | bytes 6291460
  260.2 7.2 %copy-start.7 = (f32[16,4,8,8]{3,1,2,0:T(4,128)}, f32[16,4,8,8]{3,1,2,0:T(4,128)S(1)}, u32[]{:S(2)}) copy-start(f32[16,4,8,8]{3,1,2,0:T(4,128)S(1)} %get-tuple-element.42) | copy-start | bytes 49156
  260.4 2.2 copy-start.14
  267.4 4.2 copy-start.9
  275.5 1.1 copy-start.11
  275.5 9.8 %copy-start.4 = (f32[16,8,128,4,8]{2,4,3,1,0:T(8,128)}, f32[16,8,128,4,8]{2,4,3,1,0:T(8,128)S(1)}, u32[]{:S(2)}) copy-start(f32[16,8,128,4,8]{2,4,3,1,0:T(8,128)S(1)} %get-tuple-element.39) | copy-start | bytes 6291460
  276.6 3.2 copy-start.13
  285.3 3.9 copy-start.8
  289.2 5.4 %copy-start = (bf16[16,128,1024]{1,2,0:T(8,128)(2,1)S(1)}, bf16[16,128,1024]{1,2,0:T(8,128)(2,1)}, u32[]{:S(2)}) copy-start(bf16[16,128,1024]{1,2,0:T(8,128)(2,1)} %copy.370) | copy-start | bytes 12582916
  289.2 5.4 %copy-start.3 = (f32[16,8,128,4,8]{2,4,3,1,0:T(8,128)S(1)}, f32[16,8,128,4,8]{2,4,3,1,0:T(8,128)}, u32[]{:S(2)}) copy-start(f32[16,8,128,4,8]{2,4,3,1,0:T(8,128)} %get-tuple-element.41) | copy-start | bytes 6291460
  289.2 5.4 %copy-start.10 = (f32[16,4,8,8]{3,1,2,0:T(4,128)S(1)}, f32[16,4,8,8]{3,1,2,0:T(4,128)}, u32[]{:S(2)}) copy-start(f32[16,4,8,8]{3,1,2,0:T(4,128)} %copy-done.9) | copy-start | bytes 49156
  289.2 5.4 %copy-start.17 = (f32[16,4,8,8]{3,1,2,0:T(4,128)S(1)}, f32[16,4,8,8]{3,1,2,0:T(4,128)}, u32[]{:S(2)}) copy-start(f32[16,4,8,8]{3,1,2,0:T(4,128)} %broadcast_maximum_fusion.1) | copy-start | bytes 49156
  294.6 3.5 copy-start.1
  294.6 3.5 copy-start.5
  294.6 3.5 copy-start.12
  294.6 3.5 copy-start.18
  298.1 3.4 copy-start.15
  298.1 3.4 copy-start.16
  298.1 9.9 %copy-start.6 = (f32[16,4,8,8]{3,1,2,0:T(4,128)S(1)}, f32[16,4,8,8]{3,1,2,0:T(4,128)}, u32[]{:S(2)}) copy-start(f32[16,4,8,8]{3,1,2,0:T(4,128)} %get-tuple-element.44) | copy-start | bytes 49156
  302.5 24.7 %all-to-all-start.1 = ((f32[32,2,256]{2,1,0:T(2,128)}), f32[32,2,256]{2,1,0:T(2,128)S(1)}, u32[]{:S(2)}, u32[]{:S(2)}) async-start(f32[32,2,256]{2,1,0:T(2,128)} %reshape.319), calls=%async_computation.1 | async-start | bytes 131072 | tf_op jit(solution)/shard_map/all_to_all | solution.py:168
  327.2 24.9 %all-to-all-start.3 = ((f32[32,2,256]{2,1,0:T(2,128)}), f32[32,2,256]{2,1,0:T(2,128)S(1)}, u32[]{:S(2)}, u32[]{:S(2)}) async-start(f32[32,2,256]{2,1,0:T(2,128)} %reshape.328), calls=%async_computation.3 | async-start | bytes 131072 | tf_op jit(solution)/shard_map/all_to_all | solution.py:169
  352.1 9.7 %copy-start.20 = (s32[8,4]{0,1:T(4,128)S(1)}, s32[8,4]{0,1:T(4,128)}, u32[]{:S(2)}) copy-start(s32[8,4]{0,1:T(4,128)} %param.11) | copy-start | bytes 388
  352.1 83.7 %all-to-all-start.4 = ((bf16[32,2,32768]{2,1,0:T(2,128)(2,1)}), bf16[32,2,32768]{2,1,0:T(2,128)(2,1)}, u32[]{:S(2)}, u32[]{:S(2)}) async-start(bf16[32,2,32768]{2,1,0:T(2,128)(2,1)} %reshape.337), calls=%async_computation.4 | async-start | bytes 8388608 | tf_op jit(solution)/shard_map/all_to_all | solution.py:166
Sparse Core Ops, SparseCore 0:
  23.9 141.7 all-gather.2
where the time goes:
time: 518 us; the launch traced here: 513 us
  local copies, waits for them, and re-layouts  188 us (36%)
  blocking collectives  145 us (28%)
  matrix products  63.8 us (12%)
  waiting for transfers between devices  47.1 us (9%)
  starting transfers between devices  29.4 us (6%)
  other arithmetic  25 us (5%)
  between operations  14.9 us (3%)
    slice x8, local copies, waits for them, and re-layouts, item_partial(): value_rows = panel_rows[:, KVH * HD:].reshape(token_count, KVH, HD)  50 us
    all_to_all x1, waiting for transfers between devices, per_device(): lax.all_to_all(part_out, 'cache', split_axis=0, concat_axis=0, tiled=True)  47.1 us
    all_gather x1, blocking collectives, per_device(): lax.all_gather(page_owner, 'cache', axis=0, tiled=True)  42.9 us
    all_gather x1, blocking collectives, per_device(): lax.all_gather(page_index, 'cache', axis=0, tiled=True)  37.2 us
    all_to_all x1, blocking collectives, per_device(): lax.all_to_all(result_rows, 'grp', split_axis=0, concat_axis=0, tiled=True)  34.8 us
    gather x4, local copies, waits for them, and re-layouts, owner_work(): kv_cache[meta_part[:, 1:]].reshape(finish - offset, -1, kv_cache.shape[2])  32.6 us
    slice x4, local copies, waits for them, and re-layouts, item_partial(): key_rows = panel_rows[:, :KVH * HD].reshape(token_count, KVH, HD)  25.6 us
    dot_general x4, matrix products, item_partial(): jnp.einsum('tkgu,ukd->tkgd', weights.astype(jnp.bfloat16), value_rows, pr...  20.2 us
  transfers between devices with their start and end apart: 5, of which 1 were waited for; matrix products, arithmetic and copies ran while one was open for 47% of the time, Pallas kernels for 0%

commit v1 on v0

v1 whole, which is shorter than its diff:
```python
import math

import jax
import jax.numpy as jnp
from jax import lax
from jax.experimental import pallas as pl
from jax.experimental.pallas import tpu as pltpu
from jax.sharding import PartitionSpec as P

KVH = 8
HD = 128
GQ = 8
STEPS = 4
PAGE = 128
SEL = 4
NX = 4
NZ = 8
NG = 8
NC = NX * NZ
REQ = 8
CAP = 2
PAGES = 16
GROUP = STEPS * GQ
ROWS = KVH * GROUP
HALF = REQ // 2
NEG = -1e30
SCALE = 1.0 / math.sqrt(HD)
BF16 = jnp.bfloat16
F32 = jnp.float32
I32 = jnp.int32

L_REQ, L_PAGE, L_TOK = 0, 2, 4


def rows_to_lanes(column, eye):
    wide = jnp.broadcast_to(column, (ROWS, 128))
    top = jnp.sum(jnp.where(eye, wide[:128], 0.0), axis=0, keepdims=True)
    low = jnp.sum(jnp.where(eye, wide[128:], 0.0), axis=0, keepdims=True)
    return top, low


def lanes_to_rows(pair, eye):
    top = jnp.sum(jnp.where(eye, jnp.broadcast_to(pair[0:1], (128, 128)), 0.0), axis=1, keepdims=True)
    low = jnp.sum(jnp.where(eye, jnp.broadcast_to(pair[1:2], (128, 128)), 0.0), axis=1, keepdims=True)
    return jnp.concatenate([top, low], axis=0)


def kernel(
    q_ref,
    new_ref,
    rowtab_ref,
    coltab_ref,
    kv_hbm,
    out_ref,
    kv_ref,
    ag0,
    ag1,
    ag2,
    ag3,
    ag4,
    ag5,
    ag6,
    ag7,
    newv,
    xsend,
    recvq,
    outb,
    retb,
    stato,
    statb,
    plan_out,
    plan_in,
    midx_v,
    plan_s,
    midx_s,
    newmix,
    newstat,
    fin,
    kv_sem,
    loc_sem,
    gq_send,
    gq_recv,
    gn_send,
    gn_recv,
    pl_send,
    pl_recv,
    r_send,
    l_send,
    ag_recv,
    x_send,
    x_recv,
    o_send,
    o_recv,
    s_send,
    s_recv,
    f_send,
    f_recv,
):
    ag = [ag0, ag1, ag2, ag3, ag4, ag5, ag6, ag7]
    g = lax.axis_index("grp")
    c = lax.axis_index("cache")
    mx, mz = c // NZ, c % NZ

    def node(x, z):
        return {"cache": (x % NX) * NZ + z % NZ}

    kv_copy = pltpu.make_async_copy(kv_hbm, kv_ref, kv_sem)
    kv_copy.start()

    barrier = pltpu.get_barrier_semaphore()

    @pl.loop(1, NG)
    def _(i):
        pl.semaphore_signal(barrier, inc=1, device_id={"grp": (g + i) % NG})

    @pl.loop(1, NC)
    def _(i):
        pl.semaphore_signal(barrier, inc=1, device_id={"cache": (c + i) % NC})

    lane = lax.broadcasted_iota(I32, (NZ * 8, 128), 1)
    row = lax.broadcasted_iota(I32, (NZ * 8, 128), 0)
    owner_id = (row % 8) * NZ + row // 8
    match = (rowtab_ref[0:1, :] == owner_id) & (lane < NC)
    first = jnp.min(jnp.where(match, lane, 999), axis=1, keepdims=True)
    last = jnp.max(jnp.where(match, lane, -1), axis=1, keepdims=True)
    is0 = lane == first
    is1 = match & (lane == last) & (last > first)
    page_row = jnp.broadcast_to(rowtab_ref[1:2, :], (NZ * 8, 128))
    tok_row = jnp.broadcast_to(rowtab_ref[2:3, :], (NZ * 8, 128))
    plan = jnp.zeros((NZ * 8, 128), I32)
    for slot, here in enumerate((is0, is1)):
        for base, value in ((L_REQ, lane // SEL), (L_PAGE, page_row), (L_TOK, tok_row)):
            picked = jnp.sum(jnp.where(here, value, 0), axis=1, keepdims=True)
            plan = jnp.where(lane == base + slot, picked, plan)
    plan_out[...] = plan.reshape(NZ, 8, 128)

    e_lane = lax.broadcasted_iota(I32, (NC, 128), 1)
    e_row = lax.broadcasted_iota(I32, (NC, 128), 0)
    owner_col = coltab_ref[...]
    earlier = (owner_col == rowtab_ref[0:1, :]) & (e_lane < e_row)
    rank = jnp.max(jnp.where(earlier, 1, 0), axis=1, keepdims=True)
    hop = (owner_col % NZ + NZ - mz) % NZ
    dxs = (owner_col // NZ + NX - mx) % NX
    midx_v[...] = (hop * NX + dxs) * CAP + rank

    pl.semaphore_wait(barrier, NG - 1 + NC - 1)

    def gq_copy(i):
        return pltpu.make_async_remote_copy(
            q_ref.at[(g + i) % NG], ag0.at[g], gq_send.at[i], gq_recv.at[i], device_id={"grp": (g + i) % NG}
        )

    def gq_arrival(i):
        src = (g + NG - i) % NG
        return pltpu.make_async_remote_copy(
            q_ref.at[src], ag0.at[src], gq_send.at[i], gq_recv.at[i], device_id={"grp": (g + i) % NG}
        )

    def gn_copy(i):
        return pltpu.make_async_remote_copy(
            new_ref.at[(g + i) % NG], newv.at[g], gn_send.at[i], gn_recv.at[i], device_id={"grp": (g + i) % NG}
        )

    def gn_arrival(i):
        src = (g + NG - i) % NG
        return pltpu.make_async_remote_copy(
            new_ref.at[src], newv.at[src], gn_send.at[i], gn_recv.at[i], device_id={"grp": (g + i) % NG}
        )

    @pl.loop(1, NG)
    def _(i):
        gq_copy(i).start()

    own_q = pltpu.make_async_copy(q_ref.at[g], ag0.at[g], loc_sem.at[0])
    own_n = pltpu.make_async_copy(new_ref.at[g], newv.at[g], loc_sem.at[1])
    own_q.start()
    own_n.start()

    @pl.loop(1, NG)
    def _(i):
        gn_copy(i).start()

    def plan_copy(i):
        k, dx = i // NX, i % NX
        return pltpu.make_async_remote_copy(
            plan_out.at[(mz + k) % NZ], plan_in.at[i], pl_send.at[i], pl_recv.at[i], device_id=node(mx + dx, mz + k)
        )

    @pl.loop(1, NC)
    def _(i):
        plan_copy(i).start()

    own_p = pltpu.make_async_copy(plan_out.at[mz], plan_in.at[0], loc_sem.at[2])
    own_p.start()
    midx_copy = pltpu.make_async_copy(midx_v, midx_s, loc_sem.at[3])
    midx_copy.start()

    @pl.loop(1, NG)
    def _(i):
        gq_arrival(i).wait_recv()

    own_q.wait()

    def right(k, half):
        part = pl.ds(half * HALF, HALF)
        return pltpu.make_async_remote_copy(
            ag[k].at[part], ag[k + 1].at[part], r_send.at[k, half], ag_recv.at[k + 1, half], device_id=node(mx, mz + 1)
        )

    def left(k, half):
        part = pl.ds(half * HALF, HALF)
        to = (k - 1) % NZ
        return pltpu.make_async_remote_copy(
            ag[k].at[part], ag[to].at[part], l_send.at[k, half], ag_recv.at[to, half], device_id=node(mx, mz + NZ - 1)
        )

    moves = []

    def go(copy):
        copy.start()
        moves.append(copy)

    go(right(0, 0))
    go(left(0, 1))
    go(right(0, 1))
    go(left(0, 0))

    @pl.loop(1, NC)
    def _(i):
        plan_copy(i).wait_recv()

    own_p.wait()
    plan_read = pltpu.make_async_copy(plan_in, plan_s, loc_sem.at[4])
    plan_read.start()
    plan_read.wait()

    def x_copy(k, dx):
        return pltpu.make_async_remote_copy(
            xsend.at[k, dx - 1], recvq.at[k, dx], x_send.at[k, dx], x_recv.at[k, dx], device_id=node(mx + dx, mz)
        )

    def spread(k):
        for slot in range(CAP):
            recvq[k, 0, slot] = ag[k][plan_s[k * NX, mx, L_REQ + slot]]

        @pl.loop(1, NX)
        def _(dx):
            to = (mx + dx) % NX
            for slot in range(CAP):
                xsend[k, dx - 1, slot] = ag[k][plan_s[k * NX, to, L_REQ + slot]]
            x_copy(k, dx).start()

    spread(0)

    own_n.wait()

    @pl.loop(1, NG)
    def _(i):
        gn_arrival(i).wait_recv()

    eye = lax.broadcasted_iota(I32, (128, 128), 0) == lax.broadcasted_iota(I32, (128, 128), 1)
    n_row = lax.broadcasted_iota(I32, (ROWS, STEPS * KVH), 0)
    n_col = lax.broadcasted_iota(I32, (ROWS, STEPS * KVH), 1)
    n_ok = (n_row // GROUP == n_col % KVH) & (n_col // KVH <= (n_row % GROUP) // GQ)

    @pl.loop(0, REQ)
    def _(r):
        scores = lax.dot_general(ag0[r], newv[r, 0], (((1,), (1,)), ((), ())), preferred_element_type=F32) * SCALE
        scores = jnp.where(n_ok, scores, NEG)
        top = jnp.max(scores, axis=1, keepdims=True)
        weights = jnp.where(n_ok, jnp.exp(scores - top), 0.0)
        total = jnp.sum(weights, axis=1, keepdims=True)
        newmix[r] = jnp.dot(weights.astype(BF16), newv[r, 1], preferred_element_type=F32)
        for base, column in ((0, top), (2, total)):
            upper, lower = rows_to_lanes(column, eye)
            newstat[r, base : base + 1] = upper
            newstat[r, base + 1 : base + 2] = lower

    kv_copy.wait()

    def o_copy(k, dx):
        i = k * NX + dx
        return pltpu.make_async_remote_copy(
            outb.at[i], retb.at[pl.ds(i * CAP, CAP)], o_send.at[i], o_recv.at[i],
            device_id=node(mx + NX - dx, mz + NZ - k),
        )

    def s_copy(k, dx):
        i = k * NX + dx
        return pltpu.make_async_remote_copy(
            stato.at[i], statb.at[pl.ds(i * CAP, CAP)], s_send.at[i], s_recv.at[i],
            device_id=node(mx + NX - dx, mz + NZ - k),
        )

    token = lax.broadcasted_iota(I32, (ROWS, PAGE), 1)

    def attend(k, dx):
        i = k * NX + dx
        for slot in range(CAP):
            page = plan_s[i, mx, L_PAGE + slot]
            usable = token < plan_s[i, mx, L_TOK + slot]
            query = recvq[k, dx, slot]
            scores = jnp.concatenate(
                [
                    lax.dot_general(
                        query[e * GROUP : (e + 1) * GROUP],
                        kv_ref[page, :, e * HD : (e + 1) * HD],
                        (((1,), (1,)), ((), ())),
                        preferred_element_type=F32,
                    )
                    for e in range(KVH)
                ],
                axis=0,
            )
            scores = jnp.where(usable, scores * SCALE, NEG)
            top = jnp.max(scores, axis=1, keepdims=True)
            weights = jnp.where(usable, jnp.exp(scores - top), 0.0)
            total = jnp.sum(weights, axis=1, keepdims=True)
            rounded = weights.astype(BF16)
            for e in range(KVH):
                mixed = jnp.dot(
                    rounded[e * GROUP : (e + 1) * GROUP],
                    kv_ref[page, :, (KVH + e) * HD : (KVH + e + 1) * HD],
                    preferred_element_type=F32,
                )
                outb[i, slot, e * GROUP : (e + 1) * GROUP] = mixed.astype(BF16)
            for base, column in ((0, top), (2, total)):
                upper, lower = rows_to_lanes(column, eye)
                stato[i, slot, base : base + 1] = upper
                stato[i, slot, base + 1 : base + 2] = lower

    def work(ks):
        @pl.loop(0, len(ks) * NX)
        def _(t):
            dx = t % NX
            k = ks[0] if len(ks) == 1 else jnp.where(t < NX, ks[0], ks[1])

            @pl.when(dx > 0)
            def _():
                x_copy(k, dx).wait_recv()

            attend(k, dx)

            @pl.when(k + dx > 0)
            def _():
                o_copy(k, dx).start()
                s_copy(k, dx).start()

    steps = [(0,), (1, 7), (2, 6), (3, 5), (4,)]
    for step in range(1, 5):
        for half_a, half_b in ((0, 1), (1, 0)):
            if step < 4:
                right(step - 1, half_a).wait_recv()
                if step + 1 < 4 or half_a == 0:
                    go(right(step, half_a))
                left((NZ - step + 1) % NZ, half_b).wait_recv()
                if step + 1 < 4 or half_b == 1:
                    go(left(NZ - step, half_b))
        if step == 4:
            right(3, 0).wait_recv()
            left(5, 1).wait_recv()
        for k in steps[step]:
            spread(k)
        work(steps[step - 1])
    work(steps[4])

    own_o = pltpu.make_async_copy(outb.at[0], retb.at[pl.ds(0, CAP)], loc_sem.at[5])
    own_s = pltpu.make_async_copy(stato.at[0], statb.at[pl.ds(0, CAP)], loc_sem.at[6])
    own_o.start()
    own_s.start()
    midx_copy.wait()
    own_o.wait()
    own_s.wait()

    @pl.loop(1, NC)
    def _(i):
        o_copy(i // NX, i % NX).wait_recv()
        s_copy(i // NX, i % NX).wait_recv()

    def f_copy(i):
        to = (g + i) % NG
        return pltpu.make_async_remote_copy(
            fin.at[to], out_ref.at[g], f_send.at[i], f_recv.at[i], device_id={"grp": to}
        )

    def f_arrival(i):
        src = (g + NG - i) % NG
        return pltpu.make_async_remote_copy(
            fin.at[src], out_ref.at[src], f_send.at[i], f_recv.at[i], device_id={"grp": (g + i) % NG}
        )

    own_f = pltpu.make_async_copy(fin.at[g], out_ref.at[g], loc_sem.at[7])

    @pl.loop(0, NG)
    def _(t):
        i = (t + 1) % NG
        r = (g + i) % NG
        at = [midx_s[r * SEL + s, 0] for s in range(SEL)]
        stats = [statb[a] for a in at]
        new = newstat[r]
        peak = new[0:2]
        for stat in stats:
            peak = jnp.maximum(peak, stat[0:2])
        shares = [jnp.exp(stat[0:2] - peak) for stat in stats] + [jnp.exp(new[0:2] - peak)]
        denominator = shares[SEL] * new[2:4]
        for s in range(SEL):
            denominator = denominator + shares[s] * stats[s][2:4]
        result = lanes_to_rows(shares[SEL] / denominator, eye) * newmix[r]
        for s in range(SEL):
            result = result + lanes_to_rows(shares[s] / denominator, eye) * retb[at[s]].astype(F32)
        fin[r] = result.astype(BF16)

        @pl.when(i > 0)
        def _():
            f_copy(i).start()

        @pl.when(i == 0)
        def _():
            own_f.start()

    own_f.wait()

    for copy in moves:
        copy.wait_send()

    @pl.loop(1, NG)
    def _(i):
        gq_copy(i).wait_send()
        gn_copy(i).wait_send()

    @pl.loop(1, NC)
    def _(i):
        plan_copy(i).wait_send()
        o_copy(i // NX, i % NX).wait_send()
        s_copy(i // NX, i % NX).wait_send()

    @pl.loop(0, NZ)
    def _(k):
        for dx in range(1, NX):
            x_copy(k, dx).wait_send()

    @pl.loop(1, NG)
    def _(i):
        f_arrival(i).wait_recv()
        f_copy(i).wait_send()


def per_device(queries, new_kv, kv_cache, page_owner, page_index, lengths):
    q = queries.reshape(REQ, STEPS, KVH, GQ, HD).transpose(0, 2, 1, 3, 4).reshape(REQ, ROWS, HD)
    new = new_kv.reshape(REQ, STEPS, 2, KVH, HD).transpose(0, 2, 1, 3, 4).reshape(REQ, 2, STEPS * KVH, HD)
    starts = jnp.arange(SEL, dtype=I32) * PAGE
    counts = jnp.clip(lengths[:, None] - starts[None, :], 0, PAGE)
    owners = page_owner.reshape(1, NC)
    rows = jnp.concatenate([owners, page_index.reshape(1, NC), counts.reshape(1, NC)], axis=0)
    rowtab = jnp.pad(rows, ((0, 5), (0, 128 - NC)), constant_values=-1)
    coltab = jnp.broadcast_to(page_owner.reshape(NC, 1), (NC, 128))
    dma = pltpu.SemaphoreType.DMA
    block = pltpu.VMEM((REQ, ROWS, HD), BF16)
    vmem = pl.BlockSpec(memory_space=pltpu.VMEM)
    out = pl.pallas_call(
        kernel,
        out_shape=jax.ShapeDtypeStruct((REQ, ROWS, HD), BF16),
        in_specs=[vmem, vmem, vmem, vmem, pl.BlockSpec(memory_space=pl.ANY)],
        out_specs=pl.BlockSpec(memory_space=pl.ANY),
        scratch_shapes=[
            pltpu.VMEM((PAGES, PAGE, 2 * KVH * HD), BF16),
            *[block] * NZ,
            pltpu.VMEM((REQ, 2, STEPS * KVH, HD), BF16),
            pltpu.VMEM((NZ, NX - 1, CAP, ROWS, HD), BF16),
            pltpu.VMEM((NZ, NX, CAP, ROWS, HD), BF16),
            pltpu.VMEM((NC, CAP, ROWS, HD), BF16),
            pltpu.VMEM((NC * CAP, ROWS, HD), BF16),
            pltpu.VMEM((NC, CAP, 8, 128), F32),
            pltpu.VMEM((NC * CAP, 8, 128), F32),
            pltpu.VMEM((NZ, 8, 128), I32),
            pltpu.VMEM((NC, 8, 128), I32),
            pltpu.VMEM((NC, 128), I32),
            pltpu.SMEM((NC, 8, 128), I32),
            pltpu.SMEM((NC, 128), I32),
            pltpu.VMEM((REQ, ROWS, HD), F32),
            pltpu.VMEM((REQ, 8, 128), F32),
            block,
            dma,
            dma((8,)),
            dma((NG,)),
            dma((NG,)),
            dma((NG,)),
            dma((NG,)),
            dma((NC,)),
            dma((NC,)),
            dma((NZ, 2)),
            dma((NZ, 2)),
            dma((NZ, 2)),
            dma((NZ, NX)),
            dma((NZ, NX)),
            dma((NC,)),
            dma((NC,)),
            dma((NC,)),
            dma((NC,)),
            dma((NG,)),
            dma((NG,)),
        ],
        compiler_params=pltpu.CompilerParams(
            collective_id=0, has_side_effects=True, vmem_limit_bytes=56 * 1024 * 1024
        ),
        name="paged_decode",
    )(q, new, rowtab, coltab, kv_cache)
    out = out.reshape(REQ, KVH, STEPS, GQ, HD).transpose(0, 2, 1, 3, 4)
    return out.reshape(REQ, STEPS, KVH * GQ * HD)


def solution(mesh):
    in_specs = (
        P(("grp", "cache"), None, None),
        P(("grp", "cache"), None, None),
        P(("grp", "cache"), None, None),
        P(("grp", "cache"), None),
        P(("grp", "cache"), None, None),
        P(("grp", "cache")),
    )
    out_specs = P(("grp", "cache"), None, None)
    return jax.shard_map(
        per_device, mesh=mesh, in_specs=in_specs, out_specs=out_specs, check_vma=False
    )
```

time: 518 us -> 189 us (0.36)
  local copies, waits for them, and re-layouts: 188 us -> 9.32 us
  Pallas kernels: 0 us -> 178 us
  blocking collectives: 145 us -> 0 us
  matrix products: 63.8 us -> 0 us
  waiting for transfers between devices: 47.1 us -> 0 us
  starting transfers between devices: 29.4 us -> 0 us
  other arithmetic: 25 us -> 0.74 us
  between operations: 14.9 us -> 0.03 us
    pallas_call x0 -> x1, Pallas kernels: none -> 178 us  [per_device(): pl.pallas_call(kernel, out_shape=jax.ShapeDtypeStruct((REQ, ROWS, HD), BF...]
    slice x22 -> x0, local copies, waits for them, and re-layouts: 80.3 us -> none  [the longest x8 50 us: item_partial(): value_rows = panel_rows[:, KVH * HD:].reshape(token_count, KVH, HD)]
    all_gather x2 -> x0, blocking collectives: 80.1 us -> none  [the longest x1 42.9 us: per_device(): lax.all_gather(page_owner, 'cache', axis=0, tiled=True)]
    dot_general x12 -> x0, matrix products: 63.8 us -> none  [the longest x4 20.2 us: item_partial(): jnp.einsum('tkgu,ukd->tkgd', weights.astype(jnp.bfloat16), value_rows, pr...]
    all_to_all x2 -> x0, blocking collectives: 50.9 us -> none  [the longest x1 34.8 us: per_device(): lax.all_to_all(result_rows, 'grp', split_axis=0, concat_axis=0, tiled=True)]
    all_to_all x4 -> x0, waiting for transfers between devices: 47.1 us -> none  [the longest x1 47.1 us: per_device(): lax.all_to_all(part_out, 'cache', split_axis=0, concat_axis=0, tiled=True)]
    gather x10 -> x0, local copies, waits for them, and re-layouts: 36.4 us -> none  [the longest x4 32.6 us: owner_work(): kv_cache[meta_part[:, 1:]].reshape(finish - offset, -1, kv_cache.shape[2])]
    all_to_all x4 -> x0, starting transfers between devices: 29.4 us -> none  [the longest x1 9.7 us: per_device(): lax.all_to_all(part_out, 'cache', split_axis=0, concat_axis=0, tiled=True)]
  transfers between devices with their start and end apart: 5 -> 0, of which waited for: 1 -> 0; matrix products, arithmetic and copies ran while one was open for 47% -> 0% of each run, Pallas kernels for 0% -> 0%
where the time goes in v1:
time: 189 us; the launch traced here: 188 us
  Pallas kernels  178 us (94%)
  local copies, waits for them, and re-layouts  9.32 us (5%)
    pallas_call x1, Pallas kernels, per_device(): pl.pallas_call(kernel, out_shape=jax.ShapeDtypeStruct((REQ, ROWS, HD), BF...  178 us

profile of v1, /device:TPU:1, one launch (start us, length us, event | category | flops | bytes accessed | tf_op | source)
XLA Modules:
  0.0 187.9 jit_solution(14560848638448846554)
XLA Ops:
  0.0 0.7 subtract_clamp_fusion
  0.7 0.1 min.12
  0.8 0.8 copy.15
  1.6 0.1 broadcast_in_dim.4
  1.7 0.1 reshape.64
  1.7 0.8 copy.16
  2.5 0.1 reshape.65
  2.6 0.6 pad.4.rowtab_ref
  3.2 0.7 broadcast_in_dim.10.coltab_ref
  3.9 1.0 reshape.62
  4.9 0.7 copy.20
  5.5 1.6 reshape.60
  7.1 0.9 copy.13
  8.0 177.8 %paged_decode.1 = bf16[8,256,128]{2,1,0:T(8,128)(2,1)} custom-call(bf16[8,256,128]{2,1,0:T(8,128)(2,1)} %bitcast.15, bf16[8,2,32,128]{3,2,1,0:T(8,128)(2,1)} %bitcast.17, s32[8,128]{1,0:T(8,128)} %pad.4.rowtab_ref, s32[32,128]{1,0:T(8,128)} %broadcast_in_dim.10.coltab_ref, bf16[16,128,2048]{2,1,0:T(8,128)(2,1)} %kv_hbm.1), custom_call_target="tpu_custom_call" | custom-call | tf_op jit(solution)/shard_map/paged_decode/pallas_call | solution.py:460
  185.8 1.2 copy.18
  186.9 0.9 reshape.67
  (2 shorter events, 0.0 us)

commit v2 on v1

--- a/solution.py
+++ b/solution.py
@@ -29,7 +29,7 @@
 F32 = jnp.float32
 I32 = jnp.int32
 
-L_REQ, L_PAGE, L_TOK = 0, 2, 4
+L_REQ, L_PAGE, L_TOK, L_ID = 0, 2, 4, 6
 
 
 def rows_to_lanes(column, eye):
@@ -49,54 +49,24 @@
     q_ref,
     new_ref,
     rowtab_ref,
-    coltab_ref,
     kv_hbm,
     out_ref,
     kv_ref,
-    ag0,
-    ag1,
-    ag2,
-    ag3,
-    ag4,
-    ag5,
-    ag6,
-    ag7,
-    newv,
-    xsend,
-    recvq,
-    outb,
-    retb,
-    stato,
-    statb,
-    plan_out,
-    plan_in,
-    midx_v,
-    plan_s,
-    midx_s,
-    newmix,
-    newstat,
-    fin,
-    kv_sem,
-    loc_sem,
-    gq_send,
-    gq_recv,
-    gn_send,
-    gn_recv,
-    pl_send,
-    pl_recv,
-    r_send,
-    l_send,
-    ag_recv,
-    x_send,
-    x_recv,
-    o_send,
-    o_recv,
-    s_send,
-    s_recv,
-    f_send,
-    f_recv,
+    *rest,
 ):
-    ag = [ag0, ag1, ag2, ag3, ag4, ag5, ag6, ag7]
+    rest = list(rest)
+
+    def take(count):
+        front = rest[:count]
+        del rest[:count]
+        return front
+
+    ag, xret, xstat, dense, dstat = take(NZ), take(NZ), take(NZ), take(NZ), take(NZ)
+    chain, cstat = take(NZ + 1), take(NZ + 1)
+    (newv, xsend, recvq, outb, stato, plan_out, plan_in, plan_s, newmix, newstat, fin, kv_sem, loc_sem) = take(13)
+    (gq_send, gq_recv, gn_send, gn_recv, pl_send, pl_recv, r_send, l_send, ag_recv, x_send, x_recv) = take(11)
+    (o_send, o_recv, s_send, s_recv, c_send, c_recv, cs_send, cs_recv, f_send, f_recv) = take(10)
+    ag0 = ag[0]
     g = lax.axis_index("grp")
     c = lax.axis_index("cache")
     mx, mz = c // NZ, c % NZ
@@ -132,16 +102,9 @@
         for base, value in ((L_REQ, lane // SEL), (L_PAGE, page_row), (L_TOK, tok_row)):
             picked = jnp.sum(jnp.where(here, value, 0), axis=1, keepdims=True)
             plan = jnp.where(lane == base + slot, picked, plan)
+        found = jnp.max(jnp.where(here, lane // SEL, -1), axis=1, keepdims=True)
+        plan = jnp.where(lane == L_ID + slot, found, plan)
     plan_out[...] = plan.reshape(NZ, 8, 128)
-
-    e_lane = lax.broadcasted_iota(I32, (NC, 128), 1)
-    e_row = lax.broadcasted_iota(I32, (NC, 128), 0)
-    owner_col = coltab_ref[...]
-    earlier = (owner_col == rowtab_ref[0:1, :]) & (e_lane < e_row)
-    rank = jnp.max(jnp.where(earlier, 1, 0), axis=1, keepdims=True)
-    hop = (owner_col % NZ + NZ - mz) % NZ
-    dxs = (owner_col // NZ + NX - mx) % NX
-    midx_v[...] = (hop * NX + dxs) * CAP + rank
 
     pl.semaphore_wait(barrier, NG - 1 + NC - 1)
 
@@ -192,8 +155,6 @@
 
     own_p = pltpu.make_async_copy(plan_out.at[mz], plan_in.at[0], loc_sem.at[2])
     own_p.start()
-    midx_copy = pltpu.make_async_copy(midx_v, midx_s, loc_sem.at[3])
-    midx_copy.start()
 
     @pl.loop(1, NG)
     def _(i):
@@ -279,17 +240,13 @@
     kv_copy.wait()
 
     def o_copy(k, dx):
-        i = k * NX + dx
-        return pltpu.make_async_remote_copy(
-            outb.at[i], retb.at[pl.ds(i * CAP, CAP)], o_send.at[i], o_recv.at[i],
-            device_id=node(mx + NX - dx, mz + NZ - k),
+        return pltpu.make_async_remote_copy(
+            outb.at[k, dx], xret[k].at[dx - 1], o_send.at[k, dx], o_recv.at[k, dx], device_id=node(mx + NX - dx, mz)
         )
 
     def s_copy(k, dx):
-        i = k * NX + dx
-        return pltpu.make_async_remote_copy(
-            stato.at[i], statb.at[pl.ds(i * CAP, CAP)], s_send.at[i], s_recv.at[i],
-            device_id=node(mx + NX - dx, mz + NZ - k),
+        return pltpu.make_async_remote_copy(
+            stato.at[k, dx], xstat[k].at[dx - 1], s_send.at[k, dx], s_recv.at[k, dx], device_id=node(mx + NX - dx, mz)
         )
 
     token = lax.broadcasted_iota(I32, (ROWS, PAGE), 1)
@@ -323,28 +280,26 @@
                     kv_ref[page, :, (KVH + e) * HD : (KVH + e + 1) * HD],
                     preferred_element_type=F32,
                 )
-                outb[i, slot, e * GROUP : (e + 1) * GROUP] = mixed.astype(BF16)
+                outb[k, dx, slot, e * GROUP : (e + 1) * GROUP] = mixed.astype(BF16)
             for base, column in ((0, top), (2, total)):
                 upper, lower = rows_to_lanes(column, eye)
-                stato[i, slot, base : base + 1] = upper
-                stato[i, slot, base + 1 : base + 2] = lower
-
-    def work(ks):
-        @pl.loop(0, len(ks) * NX)
-        def _(t):
-            dx = t % NX
-            k = ks[0] if len(ks) == 1 else jnp.where(t < NX, ks[0], ks[1])
-
+                stato[k, dx, slot, base : base + 1] = upper
+                stato[k, dx, slot, base + 1 : base + 2] = lower
+
+    def work(k):
+        @pl.loop(0, NX)
+        def _(dx):
             @pl.when(dx > 0)
             def _():
                 x_copy(k, dx).wait_recv()
 
             attend(k, dx)
 
-            @pl.when(k + dx > 0)
-            def _():
-                o_copy(k, dx).start()
-                s_copy(k, dx).start()
+    def give(k):
+        @pl.loop(1, NX)
+        def _(dx):
+            o_copy(k, dx).start()
+            s_copy(k, dx).start()
 
     steps = [(0,), (1, 7), (2, 6), (3, 5), (4,)]
     for step in range(1, 5):
@@ -361,21 +316,120 @@
             left(5, 1).wait_recv()
         for k in steps[step]:
             spread(k)
-        work(steps[step - 1])
-    work(steps[4])
-
-    own_o = pltpu.make_async_copy(outb.at[0], retb.at[pl.ds(0, CAP)], loc_sem.at[5])
-    own_s = pltpu.make_async_copy(stato.at[0], statb.at[pl.ds(0, CAP)], loc_sem.at[6])
-    own_o.start()
-    own_s.start()
-    midx_copy.wait()
-    own_o.wait()
-    own_s.wait()
-
-    @pl.loop(1, NC)
-    def _(i):
-        o_copy(i // NX, i % NX).wait_recv()
-        s_copy(i // NX, i % NX).wait_recv()
+        if step == 4:
+            work(3)
+            give(3)
+            work(5)
+        else:
+            for k in steps[step - 1]:
+                work(k)
+                if k == 0:
+                    give(k)
+    work(4)
+    give(4)
+    give(5)
+
+    def x_parts(k, r):
+        parts = []
+        for dx in range(NX):
+            ids = [plan_s[k * NX, (mx + dx) % NX, L_ID + slot] for slot in range(CAP)]
+            slot = jnp.where(ids[1] == r, 1, 0)
+            here = (ids[0] == r) | (ids[1] == r)
+            if dx == 0:
+                values, stat = outb[k, 0, slot], stato[k, 0, slot]
+            else:
+                values, stat = xret[k][dx - 1, slot], xstat[k][dx - 1, slot]
+            parts.append((values, jnp.where(here, stat[0:2], NEG), jnp.where(here, stat[2:4], 0.0), here))
+        return parts
+
+    def merge(parts, new):
+        peak = parts[0][1]
+        for part in parts[1:]:
+            peak = jnp.maximum(peak, part[1])
+        if new is not None:
+            peak = jnp.maximum(peak, new[1])
+        shares = []
+        total = jnp.zeros((2, 128), F32)
+        for _, top, count, here in parts:
+            share = jnp.exp(top - peak)
+            if here is not None:
+                share = jnp.where(here, share, 0.0)
+            shares.append(share)
+            total = total + share * count
+        sources = [part[0] for part in parts]
+        if new is not None:
+            share = jnp.exp(new[1] - peak)
+            total = total + share * new[2]
+            shares = [one / total for one in shares + [share]]
+            sources.append(new[0])
+        result = None
+        for share, source in zip(shares, sources):
+            term = lanes_to_rows(share, eye) * source.astype(F32)
+            result = term if result is None else result + term
+        return result, peak, total
+
+    def brought(slot, r):
+        stat = cstat[slot][r]
+        return (chain[slot][r], stat[0:2], stat[2:4], None)
+
+    def x_done(k):
+        @pl.loop(1, NX)
+        def _(dx):
+            o_copy(k, dx).wait_recv()
+            s_copy(k, dx).wait_recv()
+
+    def c_copies(k, half):
+        part = pl.ds(half * HALF, HALF)
+        inward = k - 1 if k < 4 or (k == 4 and half == 0) else k + 1
+        to = node(mx, mz + NZ - 1) if inward < k else node(mx, mz + 1)
+        return [
+            pltpu.make_async_remote_copy(
+                dense[k].at[part], chain[inward].at[part], c_send.at[k, half], c_recv.at[inward, half], device_id=to
+            ),
+            pltpu.make_async_remote_copy(
+                dstat[k].at[part], cstat[inward].at[part], cs_send.at[k, half], cs_recv.at[inward, half], device_id=to
+            ),
+        ]
+
+    def link(k):
+        x_done(k)
+        for half in range(2):
+            if k == 3 and half == 0 or k == 5 and half == 1:
+                outer = 4
+            elif k in (1, 2):
+                outer = k + 1
+            elif k in (6, 7):
+                outer = k - 1
+            else:
+                outer = None
+            if outer is not None:
+                for copy in c_copies(outer, half):
+                    copy.wait_recv()
+
+            @pl.loop(half * HALF, (half + 1) * HALF)
+            def _(r):
+                parts = x_parts(k, r)
+                if outer is not None:
+                    parts.append(brought(k, r))
+                result, peak, total = merge(parts, None)
+                dense[k][r] = result.astype(BF16)
+                dstat[k][r, 0:2] = peak
+                dstat[k][r, 2:4] = total
+
+            for copy in c_copies(k, half):
+                go(copy)
+
+    link(4)
+    give(2)
+    give(6)
+    link(3)
+    link(5)
+    give(1)
+    give(7)
+    link(2)
+    link(6)
+    link(1)
+    link(7)
 
     def f_copy(i):
         to = (g + i) % NG
@@ -390,24 +444,19 @@
         )
 
     own_f = pltpu.make_async_copy(fin.at[g], out_ref.at[g], loc_sem.at[7])
+
+    x_done(0)
+    for outer, half in ((1, 0), (1, 1), (7, 0), (7, 1)):
+        for copy in c_copies(outer, half):
+            copy.wait_recv()
 
     @pl.loop(0, NG)
     def _(t):
         i = (t + 1) % NG
         r = (g + i) % NG
-        at = [midx_s[r * SEL + s, 0] for s in range(SEL)]
-        stats = [statb[a] for a in at]
         new = newstat[r]
-        peak = new[0:2]
-        for stat in stats:
-            peak = jnp.maximum(peak, stat[0:2])
-        shares = [jnp.exp(stat[0:2] - peak) for stat in stats] + [jnp.exp(new[0:2] - peak)]
-        denominator = shares[SEL] * new[2:4]
-        for s in range(SEL):
-            denominator = denominator + shares[s] * stats[s][2:4]
-        result = lanes_to_rows(shares[SEL] / denominator, eye) * newmix[r]
-        for s in range(SEL):
-            result = result + lanes_to_rows(shares[s] / denominator, eye) * retb[at[s]].astype(F32)
+        parts = x_parts(0, r) + [brought(0, r), brought(NZ, r)]
+        result, _, _ = merge(parts, (newmix[r], new[0:2], new[2:4]))
         fin[r] = result.astype(BF16)
 
         @pl.when(i > 0)
@@ -431,13 +480,14 @@
     @pl.loop(1, NC)
     def _(i):
         plan_copy(i).wait_send()
-        o_copy(i // NX, i % NX).wait_send()
-        s_copy(i // NX, i % NX).wait_send()
-
-    @pl.loop(0, NZ)
-    def _(k):
-        for dx in range(1, NX):
+
+    for k in range(NZ):
+
+        @pl.loop(1, NX)
+        def _(dx):
             x_copy(k, dx).wait_send()
+            o_copy(k, dx).wait_send()
+            s_copy(k, dx).wait_send()
 
     @pl.loop(1, NG)
     def _(i):
@@ -453,58 +503,52 @@
     owners = page_owner.reshape(1, NC)
     rows = jnp.concatenate([owners, page_index.reshape(1, NC), counts.reshape(1, NC)], axis=0)
     rowtab = jnp.pad(rows, ((0, 5), (0, 128 - NC)), constant_values=-1)
-    coltab = jnp.broadcast_to(page_owner.reshape(NC, 1), (NC, 128))
     dma = pltpu.SemaphoreType.DMA
     block = pltpu.VMEM((REQ, ROWS, HD), BF16)
     vmem = pl.BlockSpec(memory_space=pltpu.VMEM)
     out = pl.pallas_call(
         kernel,
         out_shape=jax.ShapeDtypeStruct((REQ, ROWS, HD), BF16),
-        in_specs=[vmem, vmem, vmem, vmem, pl.BlockSpec(memory_space=pl.ANY)],
+        in_specs=[vmem, vmem, vmem, pl.BlockSpec(memory_space=pl.ANY)],
         out_specs=pl.BlockSpec(memory_space=pl.ANY),
         scratch_shapes=[
             pltpu.VMEM((PAGES, PAGE, 2 * KVH * HD), BF16),
             *[block] * NZ,
+            *[pltpu.VMEM((NX - 1, CAP, ROWS, HD), BF16)] * NZ,
+            *[pltpu.VMEM((NX - 1, CAP, 8, 128), F32)] * NZ,
+            *[block] * NZ,
+            *[pltpu.VMEM((REQ, 8, 128), F32)] * NZ,
+            *[block] * (NZ + 1),
+            *[pltpu.VMEM((REQ, 8, 128), F32)] * (NZ + 1),
             pltpu.VMEM((REQ, 2, STEPS * KVH, HD), BF16),
             pltpu.VMEM((NZ, NX - 1, CAP, ROWS, HD), BF16),
             pltpu.VMEM((NZ, NX, CAP, ROWS, HD), BF16),
-            pltpu.VMEM((NC, CAP, ROWS, HD), BF16),
-            pltpu.VMEM((NC * CAP, ROWS, HD), BF16),
-            pltpu.VMEM((NC, CAP, 8, 128), F32),
-            pltpu.VMEM((NC * CAP, 8, 128), F32),
+            pltpu.VMEM((NZ, NX, CAP, ROWS, HD), BF16),
+            pltpu.VMEM((NZ, NX, CAP, 8, 128), F32),
             pltpu.VMEM((NZ, 8, 128), I32),
             pltpu.VMEM((NC, 8, 128), I32),
-            pltpu.VMEM((NC, 128), I32),
             pltpu.SMEM((NC, 8, 128), I32),
-            pltpu.SMEM((NC, 128), I32),
             pltpu.VMEM((REQ, ROWS, HD), F32),
             pltpu.VMEM((REQ, 8, 128), F32),
             block,
             dma,
             dma((8,)),
-            dma((NG,)),
-            dma((NG,)),
-            dma((NG,)),
-            dma((NG,)),
-            dma((NC,)),
-            dma((NC,)),
+            *[dma((NG,))] * 4,
+            *[dma((NC,))] * 2,
+            *[dma((NZ, 2))] * 3,
+            *[dma((NZ, NX))] * 2,
+            *[dma((NZ, NX))] * 4,
             dma((NZ, 2)),
+            dma((NZ + 1, 2)),
             dma((NZ, 2)),
-            dma((NZ, 2)),
-            dma((NZ, NX)),
-            dma((NZ, NX)),
-            dma((NC,)),
-            dma((NC,)),
-            dma((NC,)),
-            dma((NC,)),
-            dma((NG,)),
-            dma((NG,)),
+            dma((NZ + 1, 2)),
+            *[dma((NG,))] * 2,
         ],
         compiler_params=pltpu.CompilerParams(
             collective_id=0, has_side_effects=True, vmem_limit_bytes=56 * 1024 * 1024
         ),
         name="paged_decode",
-    )(q, new, rowtab, coltab, kv_cache)
+    )(q, new, rowtab, kv_cache)
     out = out.reshape(REQ, KVH, STEPS, GQ, HD).transpose(0, 2, 1, 3, 4)
     return out.reshape(REQ, STEPS, KVH * GQ * HD)
 

time: 189 us -> 169 us (0.89)
  Pallas kernels: 178 us -> 160 us
    pallas_call x1, Pallas kernels: 178 us -> 160 us  [per_device(): pl.pallas_call(kernel, out_shape=jax.ShapeDtypeStruct((REQ, ROWS, HD), BF...]
where the time goes in v2:
time: 169 us
  Pallas kernels  160 us (95%)
  local copies, waits for them, and re-layouts  8.55 us (5%)
    pallas_call x1, Pallas kernels, per_device(): pl.pallas_call(kernel, out_shape=jax.ShapeDtypeStruct((REQ, ROWS, HD), BF...  160 us

profile of v2, /device:TPU:1, one launch (start us, length us, event | category | flops | bytes accessed | tf_op | source)
XLA Modules:
  0.0 169.0 jit_solution(15221103796280622735)
XLA Ops:
  0.0 0.7 subtract_clamp_fusion
  0.7 0.1 min.12
  0.8 0.8 copy.14
  1.6 0.1 reshape.62
  1.7 0.8 copy.15
  2.4 0.1 reshape.63
  2.5 0.6 pad.4.rowtab_ref
  3.1 1.0 reshape.60
  4.1 0.7 copy.18
  4.8 1.6 reshape.58
  6.3 0.9 copy.12
  7.2 159.7 %paged_decode.1 = bf16[8,256,128]{2,1,0:T(8,128)(2,1)} custom-call(bf16[8,256,128]{2,1,0:T(8,128)(2,1)} %bitcast.15, bf16[8,2,32,128]{3,2,1,0:T(8,128)(2,1)} %bitcast.17, s32[8,128]{1,0:T(8,128)} %pad.4.rowtab_ref, bf16[16,128,2048]{2,1,0:T(8,128)(2,1)} %kv_hbm.1), custom_call_target="tpu_custom_call" | custom-call | tf_op jit(solution)/shard_map/paged_decode/pallas_call | solution.py:509
  166.9 1.2 copy.16
  168.1 0.9 reshape.65
  (2 shorter events, 0.0 us)

commit v3 on v2

v3 whole, which is shorter than its diff:
```python
import math

import jax
import jax.numpy as jnp
from jax import lax
from jax.experimental import pallas as pl
from jax.experimental.pallas import tpu as pltpu
from jax.sharding import PartitionSpec as P

KVH = 8
HD = 128
GQ = 8
STEPS = 4
PAGE = 128
SEL = 4
NX = 4
NZ = 8
NG = 8
NC = NX * NZ
REQ = 8
CAP = 2
PAGES = 16
GROUP = STEPS * GQ
ROWS = KVH * GROUP
HALF = REQ // 2
NCH = 2
CROWS = ROWS // NCH
CHEADS = KVH // NCH
CWIDTH = CHEADS * GQ * HD
NEG = -1e30
SCALE = 1.0 / math.sqrt(HD)
BF16 = jnp.bfloat16
F32 = jnp.float32
I32 = jnp.int32

L_REQ, L_PAGE, L_TOK, L_ID = 0, 2, 4, 6


def rows_to_lanes(column, eye):
    return jnp.sum(jnp.where(eye, jnp.broadcast_to(column, (CROWS, 128)), 0.0), axis=0, keepdims=True)


def lanes_to_rows(line, eye):
    return jnp.sum(jnp.where(eye, jnp.broadcast_to(line, (CROWS, 128)), 0.0), axis=1, keepdims=True)


def kernel(q_ref, new_ref, owner_ref, page_ref, length_ref, kv_hbm, out_ref, kv_ref, *rest):
    rest = list(rest)

    def take(count):
        front = rest[:count]
        del rest[:count]
        return front

    def take_each(count):
        return [take(count) for _ in range(NCH)]

    ag, xret, xstat, dense, dstat = (take_each(NZ) for _ in range(5))
    chain, cstat = (take_each(NZ + 1) for _ in range(2))
    qs, newv, xsend, recvq, outb, stato, plan_out, plan_in, plan_s, own_s, newmix, newtop, newsum, fin = take(14)
    kv_sem, loc_sem, gq_send, gq_recv, gn_send, gn_recv, pl_send, pl_recv = take(8)
    ag_send, ag_recv, x_send, x_recv, o_send, o_recv, s_send, s_recv = take(8)
    c_send, c_recv, cs_send, cs_recv, f_send, f_recv = take(6)

    g = lax.axis_index("grp")
    c = lax.axis_index("cache")
    mx, mz = c // NZ, c % NZ

    def node(x, z):
        return {"cache": (x % NX) * NZ + z % NZ}

    barrier = pltpu.get_barrier_semaphore()

    @pl.loop(1, NG)
    def _(i):
        pl.semaphore_signal(barrier, inc=1, device_id={"grp": (g + i) % NG})

    @pl.loop(1, NC)
    def _(i):
        pl.semaphore_signal(barrier, inc=1, device_id={"cache": (c + i) % NC})

    kv_copy = pltpu.make_async_copy(kv_hbm, kv_ref, kv_sem)
    kv_copy.start()

    entry = lax.broadcasted_iota(I32, (1, 128), 1)
    owner_row = jnp.full((1, 128), -1, I32)
    page_row = jnp.zeros((1, 128), I32)
    tok_row = jnp.zeros((1, 128), I32)
    for r in range(REQ):
        for s in range(SEL):
            at = entry == r * SEL + s
            owner_row = jnp.where(at, owner_ref[s, r], owner_row)
            page_row = jnp.where(at, page_ref[s, r], page_row)
            tok_row = jnp.where(at, jnp.clip(length_ref[r] - s * PAGE, 0, PAGE), tok_row)

    shape = (NZ, 128)
    lane = lax.broadcasted_iota(I32, shape, 1)
    row = lax.broadcasted_iota(I32, shape, 0)
    owners = jnp.broadcast_to(owner_row, shape)
    pages = jnp.broadcast_to(page_row, shape)
    tokens = jnp.broadcast_to(tok_row, shape)
    plan = jnp.zeros(shape, I32)
    for x in range(NX):
        match = (owners == row + x * NZ) & (lane < NC)
        first = jnp.min(jnp.where(match, lane, 999), axis=1, keepdims=True)
        last = jnp.max(jnp.where(match, lane, -1), axis=1, keepdims=True)
        is0 = lane == first
        is1 = match & (lane == last) & (last > first)
        for slot, here in enumerate((is0, is1)):
            for base, value in ((L_REQ, lane // SEL), (L_PAGE, pages), (L_TOK, tokens)):
                picked = jnp.sum(jnp.where(here, value, 0), axis=1, keepdims=True)
                plan = jnp.where(lane == x * 8 + base + slot, picked, plan)
            found = jnp.max(jnp.where(here, lane // SEL, -1), axis=1, keepdims=True)
            plan = jnp.where(lane == x * 8 + L_ID + slot, found, plan)
    for z in range(NZ):
        plan_out[z] = plan[z : z + 1]
    own_plan = pltpu.make_async_copy(plan_out.at[mz], own_s, loc_sem.at[2 * NCH + 3])
    own_plan.start()

    @pl.loop(0, REQ)
    def _(r):
        wide = q_ref[r].astype(F32)
        rows = [wide[:, h * HD : (h + 1) * HD] for h in range(KVH * GQ)]
        qs[r] = jnp.concatenate(rows, axis=0).astype(BF16)

    pl.semaphore_wait(barrier, NG - 1 + NC - 1)

    def drain(ref, sem):
        pltpu.make_async_copy(ref, ref, sem).wait()

    def gq_copy(ch, i):
        part = pl.ds(ch * CROWS, CROWS)
        src, dst = (g + i) % NG, g
        return pltpu.make_async_remote_copy(
            qs.at[src, part], ag[ch][0].at[dst], gq_send, gq_recv.at[ch],
            device_id={"grp": (g + i) % NG},
        )

    def gn_copy(i):
        src, dst = (g + i) % NG, g
        return pltpu.make_async_remote_copy(
            new_ref.at[src], newv.at[dst], gn_send, gn_recv, device_id={"grp": (g + i) % NG}
        )

    def plan_copy(i):
        k, dx = i // NX, i % NX
        return pltpu.make_async_remote_copy(
            plan_out.at[(mz + k) % NZ], plan_in.at[i], pl_send, pl_recv, device_id=node(mx + dx, mz + k)
        )

    own_q = [
        pltpu.make_async_copy(qs.at[g, pl.ds(ch * CROWS, CROWS)], ag[ch][0].at[g], loc_sem.at[ch])
        for ch in range(NCH)
    ]
    own_n = pltpu.make_async_copy(new_ref.at[g], newv.at[g], loc_sem.at[NCH])
    own_p = pltpu.make_async_copy(plan_out.at[mz], plan_in.at[0], loc_sem.at[NCH + 1])
    for ch in range(NCH):
        own_q[ch].start()

        @pl.loop(1, NG)
        def _(i):
            gq_copy(ch, i).start()

        if ch == 0:
            own_p.start()

            @pl.loop(1, NC)
            def _(i):
                plan_copy(i).start()

    own_n.start()

    @pl.loop(1, NG)
    def _(i):
        gn_copy(i).start()

    def right(ch, k, half):
        part = pl.ds(half * HALF, HALF)
        return pltpu.make_async_remote_copy(
            ag[ch][k].at[part], ag[ch][k + 1].at[part], ag_send,
            ag_recv.at[ch * NZ + k + 1, half], device_id=node(mx, mz + 1),
        )

    def left(ch, k, half):
        part = pl.ds(half * HALF, HALF)
        to = (k - 1) % NZ
        return pltpu.make_async_remote_copy(
            ag[ch][k].at[part], ag[ch][to].at[part], ag_send,
            ag_recv.at[ch * NZ + to, half], device_id=node(mx, mz + NZ - 1),
        )

    def arrive(ch):
        drain(ag[ch][0].at[pl.ds(0, NG - 1)], gq_recv.at[ch])
        own_q[ch].wait()

    def begin(ch):
        right(ch, 0, 0).start()
        left(ch, 0, 1).start()
        right(ch, 0, 1).start()
        left(ch, 0, 0).start()

    def pass_on(ch, step):
        for half_a, half_b in ((0, 1), (1, 0)):
            if step < 4:
                right(ch, step - 1, half_a).wait_recv()
                if step + 1 < 4 or half_a == 0:
                    right(ch, step, half_a).start()
                left(ch, (NZ - step + 1) % NZ, half_b).wait_recv()
                if step + 1 < 4 or half_b == 1:
                    left(ch, NZ - step, half_b).start()
        if step == 4:
            right(ch, 3, 0).wait_recv()
            left(ch, 5, 1).wait_recv()

    def x_copy(ch, k, dx):
        return pltpu.make_async_remote_copy(
            xsend.at[ch, k, dx - 1], recvq.at[ch, k, dx], x_send, x_recv.at[ch * NZ + k],
            device_id=node(mx + dx, mz),
        )

    def spread(ch, k):
        def wanted(to, slot):
            at = to * 8 + L_REQ + slot
            return own_s[0, at] if k == 0 else plan_s[k * NX, 0, at]

        @pl.loop(1, NX)
        def _(dx):
            to = (mx + dx) % NX
            for slot in range(CAP):
                xsend[ch, k, dx - 1, slot] = ag[ch][k][wanted(to, slot)]
            x_copy(ch, k, dx).start()

        for slot in range(CAP):
            recvq[ch, k, 0, slot] = ag[ch][k][wanted(mx, slot)]

    eye = lax.broadcasted_iota(I32, (CROWS, 128), 0) == lax.broadcasted_iota(I32, (CROWS, 128), 1)

    def new_tokens(ch):
        n_row = lax.broadcasted_iota(I32, (CROWS, STEPS * CHEADS), 0)
        n_col = lax.broadcasted_iota(I32, (CROWS, STEPS * CHEADS), 1)
        n_ok = (n_row // GROUP == n_col // STEPS) & (n_col % STEPS <= n_row % STEPS)

        @pl.loop(0, REQ)
        def _(r):
            wide = newv[r].astype(F32)
            pieces = [wide[:, e * HD : (e + 1) * HD] for e in range(2 * KVH)]
            keys = jnp.concatenate(pieces[ch * CHEADS : (ch + 1) * CHEADS], axis=0).astype(BF16)
            values = jnp.concatenate(pieces[KVH + ch * CHEADS : KVH + (ch + 1) * CHEADS], axis=0).astype(BF16)
            scores = lax.dot_general(
                ag[ch][0][r], keys, (((1,), (1,)), ((), ())), preferred_element_type=F32
            ) * SCALE
            scores = jnp.where(n_ok, scores, NEG)
            top = jnp.max(scores, axis=1, keepdims=True)
            weights = jnp.where(n_ok, jnp.exp(scores - top), 0.0)
            total = jnp.sum(weights, axis=1, keepdims=True)
            newmix[ch, r] = jnp.dot(weights.astype(BF16), values, preferred_element_type=F32)
            newtop[ch, pl.ds(r, 1)] = rows_to_lanes(top, eye)
            newsum[ch, pl.ds(r, 1)] = rows_to_lanes(total, eye)

    def o_copy(ch, k, dx):
        return pltpu.make_async_remote_copy(
            outb.at[ch, k, dx], xret[ch][k].at[dx - 1], o_send, o_recv.at[ch * NZ + k],
            device_id=node(mx + NX - dx, mz),
        )

    def s_copy(ch, k, dx):
        return pltpu.make_async_remote_copy(
            stato.at[ch, k, dx], xstat[ch][k].at[dx - 1], s_send, s_recv.at[ch * NZ + k],
            device_id=node(mx + NX - dx, mz),
        )

    token = lax.broadcasted_iota(I32, (CROWS, PAGE), 1)

    def attend(ch, k, dx):
        i = k * NX + dx
        for slot in range(CAP):
            page = plan_s[i, 0, mx * 8 + L_PAGE + slot]
            usable = token < plan_s[i, 0, mx * 8 + L_TOK + slot]
            query = recvq[ch, k, dx, slot]
            scores = jnp.concatenate(
                [
                    lax.dot_general(
                        query[e * GROUP : (e + 1) * GROUP],
                        kv_ref[page, :, (ch * CHEADS + e) * HD : (ch * CHEADS + e + 1) * HD],
                        (((1,), (1,)), ((), ())),
                        preferred_element_type=F32,
                    )
                    for e in range(CHEADS)
                ],
                axis=0,
            )
            scores = jnp.where(usable, scores * SCALE, NEG)
            top = jnp.max(scores, axis=1, keepdims=True)
            weights = jnp.where(usable, jnp.exp(scores - top), 0.0)
            total = jnp.sum(weights, axis=1, keepdims=True)
            rounded = weights.astype(BF16)
            for e in range(CHEADS):
                at = KVH + ch * CHEADS + e
                mixed = jnp.dot(
                    rounded[e * GROUP : (e + 1) * GROUP],
                    kv_ref[page, :, at * HD : (at + 1) * HD],
                    preferred_element_type=F32,
                )
                outb[ch, k, dx, slot, e * GROUP : (e + 1) * GROUP] = mixed.astype(BF16)
            stato[ch, k, dx, slot : slot + 1] = rows_to_lanes(top, eye)
            stato[ch, k, dx, CAP + slot : CAP + slot + 1] = rows_to_lanes(total, eye)

    def work(ch, k):
        @pl.loop(0, NX)
        def _(dx):
            @pl.when(dx == 1)
            def _():
                drain(recvq.at[ch, k, pl.ds(1, NX - 1)], x_recv.at[ch * NZ + k])

            attend(ch, k, dx)

    def give(ch, k):
        @pl.loop(1, NX)
        def _(dx):
            o_copy(ch, k, dx).start()
            s_copy(ch, k, dx).start()

    def x_parts(ch, k, r):
        parts = []
        for dx in range(NX):
            ids = [plan_s[k * NX, 0, (mx + dx) % NX * 8 + L_ID + slot] for slot in range(CAP)]
            second = ids[1] == r
            slot = jnp.where(second, 1, 0)
            here = (ids[0] == r) | second
            if dx == 0:
                values, stat = outb[ch, k, 0, slot], stato[ch, k, 0]
            else:
                values, stat = xret[ch][k][dx - 1, slot], xstat[ch][k][dx - 1]
            top = jnp.where(second, stat[1:2], stat[0:1])
            count = jnp.where(second, stat[3:4], stat[2:3])
            parts.append((values, jnp.where(here, top, NEG), jnp.where(here, count, 0.0), here))
        return parts

    def merge(parts, new):
        peak = parts[0][1]
        for part in parts[1:]:
            peak = jnp.maximum(peak, part[1])
        if new is not None:
            peak = jnp.maximum(peak, new[1])
        shares = []
        total = jnp.zeros((1, 128), F32)
        for _, top, count, here in parts:
            share = jnp.exp(top - peak)
            if here is not None:
                share = jnp.where(here, share, 0.0)
            shares.append(share)
            total = total + share * count
        sources = [part[0] for part in parts]
        if new is not None:
            share = jnp.exp(new[1] - peak)
            total = total + share * new[2]
            shares = [one / total for one in shares + [share]]
            sources.append(new[0])
        result = None
        for share, source in zip(shares, sources):
            term = lanes_to_rows(share, eye) * source.astype(F32)
            result = term if result is None else result + term
        return result, peak, total

    def brought(ch, slot, half, rr):
        stat = cstat[ch][slot]
        return (
            chain[ch][slot][half * HALF + rr],
            stat[half, pl.ds(rr, 1), :],
            stat[half, pl.ds(HALF + rr, 1), :],
            None,
        )

    def x_done(ch, k):
        drain(xret[ch][k], o_recv.at[ch * NZ + k])
        drain(xstat[ch][k], s_recv.at[ch * NZ + k])

    def c_copies(ch, k, half):
        part = pl.ds(half * HALF, HALF)
        inward = k - 1 if k < 4 or (k == 4 and half == 0) else k + 1
        to = node(mx, mz + NZ - 1) if inward < k else node(mx, mz + 1)
        got = ch * (NZ + 1) + inward
        return [
            pltpu.make_async_remote_copy(
                dense[ch][k].at[part], chain[ch][inward].at[part], c_send, c_recv.at[got, half],
                device_id=to,
            ),
            pltpu.make_async_remote_copy(
                dstat[ch][k].at[half], cstat[ch][inward].at[half], cs_send, cs_recv.at[got, half],
                device_id=to,
            ),
        ]

    def link(ch, k):
        x_done(ch, k)
        for half in range(2):
            if k == 3 and half == 0 or k == 5 and half == 1:
                outer = 4
            elif k in (1, 2):
                outer = k + 1
            elif k in (6, 7):
                outer = k - 1
            else:
                outer = None
            if outer is not None:
                for copy in c_copies(ch, outer, half):
                    copy.wait_recv()

            @pl.loop(0, HALF)
            def _(rr):
                parts = x_parts(ch, k, half * HALF + rr)
                if outer is not None:
                    parts.append(brought(ch, k, half, rr))
                result, peak, total = merge(parts, None)
                dense[ch][k][half * HALF + rr] = result.astype(BF16)
                dstat[ch][k][half, pl.ds(rr, 1), :] = peak
                dstat[ch][k][half, pl.ds(HALF + rr, 1), :] = total

            for copy in c_copies(ch, k, half):
                copy.start()

    def f_copy(ch, i):
        part = pl.ds(ch * CWIDTH, CWIDTH)
        src, dst = (g + i) % NG, g
        return pltpu.make_async_remote_copy(
            fin.at[ch, src], out_ref.at[dst, :, part], f_send, f_recv,
            device_id={"grp": (g + i) % NG},
        )

    own_f = [
        pltpu.make_async_copy(fin.at[ch, g], out_ref.at[g, :, pl.ds(ch * CWIDTH, CWIDTH)], loc_sem.at[NCH + 3 + ch])
        for ch in range(NCH)
    ]

    def finish(ch):
        x_done(ch, 0)
        for outer, half in ((1, 0), (1, 1), (7, 0), (7, 1)):
            for copy in c_copies(ch, outer, half):
                copy.wait_recv()

        @pl.loop(1, NG + 1)
        def _(i):
            r = (g + i) % NG
            half, rr = r // HALF, r % HALF
            parts = x_parts(ch, 0, r) + [brought(ch, 0, half, rr), brought(ch, NZ, half, rr)]
            new = (newmix[ch, r], newtop[ch, pl.ds(r, 1), :], newsum[ch, pl.ds(r, 1), :])
            result, _, _ = merge(parts, new)
            pieces = [result[h * STEPS : (h + 1) * STEPS] for h in range(CHEADS * GQ)]
            fin[ch, r] = jnp.concatenate(pieces, axis=1).astype(BF16)

            @pl.when(i < NG)
            def _():
                f_copy(ch, i).start()

            @pl.when(i == NG)
            def _():
                own_f[ch].start()

    steps = [(0,), (1, 7), (2, 6), (3, 5), (4,)]

    def forward(ch, step, todo):
        pass_on(ch, step)
        if step == 3 and ch + 1 < NCH:
            begin(ch + 1)
        for k in steps[step]:
            spread(ch, k)
        for one, k in todo:
            work(one, k)

    arrive(0)
    begin(0)
    own_plan.wait()
    spread(0, 0)
    arrive(1)
    spread(1, 0)
    pass_on(0, 1)

    drain(plan_in.at[pl.ds(0, NC - 1)], pl_recv)
    own_p.wait()
    plan_read = pltpu.make_async_copy(plan_in, plan_s, loc_sem.at[NCH + 2])
    plan_read.start()
    plan_read.wait()
    spread(0, 1)
    spread(0, 7)
    kv_copy.wait()
    work(0, 0)
    give(0, 0)
    forward(0, 2, [(1, 0)])
    own_n.wait()

    drain(newv.at[pl.ds(0, NG - 1)], gn_recv)
    forward(0, 3, [(0, 1), (0, 7)])
    forward(0, 4, [(0, 2), (0, 6)])
    forward(1, 1, [(0, 3), (0, 5)])
    forward(1, 2, [(0, 4)])
    give(0, 4)
    give(0, 3)
    give(0, 5)
    forward(1, 3, [(1, 1), (1, 7)])
    new_tokens(0)
    link(0, 4)
    forward(1, 4, [(1, 2), (1, 6)])
    give(0, 2)
    give(0, 6)
    link(0, 3)
    link(0, 5)
    work(1, 3)
    work(1, 5)
    give(0, 1)
    give(0, 7)
    link(0, 2)
    link(0, 6)
    work(1, 4)
    give(1, 4)
    give(1, 3)
    give(1, 5)
    link(0, 1)
    link(0, 7)
    link(1, 4)
    give(1, 2)
    give(1, 6)
    new_tokens(1)
    link(1, 3)
    link(1, 5)
    give(1, 1)
    give(1, 7)
    give(1, 0)
    finish(0)
    link(1, 2)
    link(1, 6)
    link(1, 1)
    link(1, 7)
    finish(1)

    for ch in range(NCH):
        own_f[ch].wait()
    drain(out_ref.at[pl.ds(0, NG - 1)], f_recv)
    drain(qs.at[pl.ds(0, NG - 1)], gq_send)
    drain(newv.at[pl.ds(0, NG - 1)], gn_send)
    drain(plan_in.at[pl.ds(0, NC - 1)], pl_send)
    drain(recvq.at[:, pl.ds(0, NZ - 1)], ag_send)
    drain(xsend, x_send)
    drain(xsend, o_send)
    drain(stato.at[:, :, pl.ds(1, NX - 1)], s_send)
    drain(recvq.at[:, pl.ds(0, NZ - 1)], c_send)
    drain(newmix.at[0, pl.ds(0, NZ - 1), pl.ds(0, 16 * NCH)], cs_send)
    drain(fin.at[:, pl.ds(0, NG - 1)], f_send)


def per_device(queries, new_kv, kv_cache, page_owner, page_index, lengths):
    dma = pltpu.SemaphoreType.DMA
    vmem = pl.BlockSpec(memory_space=pltpu.VMEM)
    smem = pl.BlockSpec(memory_space=pltpu.SMEM)
    hbm = pl.BlockSpec(memory_space=pl.ANY)
    block = pltpu.VMEM((REQ, CROWS, HD), BF16)
    return pl.pallas_call(
        kernel,
        out_shape=jax.ShapeDtypeStruct((REQ, STEPS, KVH * GQ * HD), BF16),
        in_specs=[vmem, vmem, smem, smem, smem, hbm],
        out_specs=hbm,
        scratch_shapes=[
            pltpu.VMEM((PAGES, PAGE, 2 * KVH * HD), BF16),
            *[block] * (NCH * NZ),
            *[pltpu.VMEM((NX - 1, CAP, CROWS, HD), BF16)] * (NCH * NZ),
            *[pltpu.VMEM((NX - 1, 2 * CAP, 128), F32)] * (NCH * NZ),
            *[block] * (NCH * NZ),
            *[pltpu.VMEM((2, 8, 128), F32)] * (NCH * NZ),
            *[block] * (NCH * (NZ + 1)),
            *[pltpu.VMEM((2, 8, 128), F32)] * (NCH * (NZ + 1)),
            pltpu.VMEM((REQ, ROWS, HD), BF16),
            pltpu.VMEM((REQ, STEPS, 2 * KVH * HD), BF16),
            pltpu.VMEM((NCH, NZ, NX - 1, CAP, CROWS, HD), BF16),
            pltpu.VMEM((NCH, NZ, NX, CAP, CROWS, HD), BF16),
            pltpu.VMEM((NCH, NZ, NX, CAP, CROWS, HD), BF16),
            pltpu.VMEM((NCH, NZ, NX, 2 * CAP, 128), F32),
            pltpu.VMEM((NZ, 1, 128), I32),
            pltpu.VMEM((NC, 1, 128), I32),
            pltpu.SMEM((NC, 1, 128), I32),
            pltpu.SMEM((1, 128), I32),
            pltpu.VMEM((NCH, REQ, CROWS, HD), F32),
            pltpu.VMEM((NCH, REQ, 128), F32),
            pltpu.VMEM((NCH, REQ, 128), F32),
            pltpu.VMEM((NCH, REQ, STEPS, CWIDTH), BF16),
            dma,
            dma((2 * NCH + 4,)),
            dma,
            dma((NCH,)),
            *[dma] * 4,
            dma,
            dma((NCH * NZ, 2)),
            *[dma, dma((NCH * NZ,))] * 3,
            *[dma, dma((NCH * (NZ + 1), 2))] * 2,
            *[dma] * 2,
        ],
        compiler_params=pltpu.CompilerParams(
            collective_id=0, has_side_effects=True, vmem_limit_bytes=56 * 1024 * 1024
        ),
        name="paged_decode",
    )(queries, new_kv, page_owner.T, page_index.reshape(REQ, SEL).T, lengths, kv_cache)


def solution(mesh):
    in_specs = (
        P(("grp", "cache"), None, None),
        P(("grp", "cache"), None, None),
        P(("grp", "cache"), None, None),
        P(("grp", "cache"), None),
        P(("grp", "cache"), None, None),
        P(("grp", "cache")),
    )
    out_specs = P(("grp", "cache"), None, None)
    return jax.shard_map(
        per_device, mesh=mesh, in_specs=in_specs, out_specs=out_specs, check_vma=False
    )
```

time: 169 us -> 137 us (0.81)
  Pallas kernels: 160 us -> 135 us
  local copies, waits for them, and re-layouts: 8.55 us -> 2.02 us
    pallas_call x1, Pallas kernels: 160 us -> 135 us  [per_device(): pl.pallas_call(kernel, out_shape=jax.ShapeDtypeStruct((REQ, STEPS, KVH *...]
    reshape x7 -> x0, local copies, waits for them, and re-layouts: 5.21 us -> none  [the longest x2 2.46 us: per_device(): queries.reshape(REQ, STEPS, KVH, GQ, HD).transpose(0, 2, 1, 3, 4)]
where the time goes in v3:
time: 137 us
  Pallas kernels  135 us (99%)
  local copies, waits for them, and re-layouts  2.02 us (1%)
    pallas_call x1, Pallas kernels, per_device(): pl.pallas_call(kernel, out_shape=jax.ShapeDtypeStruct((REQ, STEPS, KVH *...  135 us

profile of v3, /device:TPU:1, one launch (start us, length us, event | category | flops | bytes accessed | tf_op | source)
XLA Modules:
  0.0 137.2 jit_solution(13147242424432662909)
XLA Ops:
  0.0 135.2 %paged_decode.1 = bf16[8,4,8192]{2,1,0:T(4,128)(2,1)} custom-call(bf16[8,4,8192]{2,1,0:T(4,128)(2,1)} %q_ref.1, bf16[8,4,2048]{2,1,0:T(4,128)(2,1)} %new_ref.1, s32[4,8]{1,0:T(4,128)} %bitcast.4, s32[4,8]{1,0:T(4,128)} %bitcast.5, s32[8]{0:T(128)} %length_ref.1, bf16[16,128,2048]{2,1,0:T(8,128)(2,1)} %kv_hbm.1), custom_call_target="tpu_custom_call" | custom-call | tf_op jit(solution)/shard_map/paged_decode/pallas_call | solution.py:556
  135.2 2.0 %copy.8 = bf16[8,4,8192]{2,1,0:T(4,128)(2,1)} copy(bf16[8,4,8192]{2,1,0:T(4,128)(2,1)} %paged_decode.1) | data formatting | bytes 1048576

commit v4 on v3

--- a/solution.py
+++ b/solution.py
@@ -82,47 +82,14 @@
     kv_copy = pltpu.make_async_copy(kv_hbm, kv_ref, kv_sem)
     kv_copy.start()
 
-    entry = lax.broadcasted_iota(I32, (1, 128), 1)
-    owner_row = jnp.full((1, 128), -1, I32)
-    page_row = jnp.zeros((1, 128), I32)
-    tok_row = jnp.zeros((1, 128), I32)
-    for r in range(REQ):
-        for s in range(SEL):
-            at = entry == r * SEL + s
-            owner_row = jnp.where(at, owner_ref[s, r], owner_row)
-            page_row = jnp.where(at, page_ref[s, r], page_row)
-            tok_row = jnp.where(at, jnp.clip(length_ref[r] - s * PAGE, 0, PAGE), tok_row)
-
-    shape = (NZ, 128)
-    lane = lax.broadcasted_iota(I32, shape, 1)
-    row = lax.broadcasted_iota(I32, shape, 0)
-    owners = jnp.broadcast_to(owner_row, shape)
-    pages = jnp.broadcast_to(page_row, shape)
-    tokens = jnp.broadcast_to(tok_row, shape)
-    plan = jnp.zeros(shape, I32)
-    for x in range(NX):
-        match = (owners == row + x * NZ) & (lane < NC)
-        first = jnp.min(jnp.where(match, lane, 999), axis=1, keepdims=True)
-        last = jnp.max(jnp.where(match, lane, -1), axis=1, keepdims=True)
-        is0 = lane == first
-        is1 = match & (lane == last) & (last > first)
-        for slot, here in enumerate((is0, is1)):
-            for base, value in ((L_REQ, lane // SEL), (L_PAGE, pages), (L_TOK, tokens)):
-                picked = jnp.sum(jnp.where(here, value, 0), axis=1, keepdims=True)
-                plan = jnp.where(lane == x * 8 + base + slot, picked, plan)
-            found = jnp.max(jnp.where(here, lane // SEL, -1), axis=1, keepdims=True)
-            plan = jnp.where(lane == x * 8 + L_ID + slot, found, plan)
-    for z in range(NZ):
-        plan_out[z] = plan[z : z + 1]
-    own_plan = pltpu.make_async_copy(plan_out.at[mz], own_s, loc_sem.at[2 * NCH + 3])
-    own_plan.start()
-
-    @pl.loop(0, REQ)
-    def _(r):
-        wide = q_ref[r].astype(F32)
-        rows = [wide[:, h * HD : (h + 1) * HD] for h in range(KVH * GQ)]
-        qs[r] = jnp.concatenate(rows, axis=0).astype(BF16)
-
+    def make_rows(ch):
+        @pl.loop(0, REQ)
+        def _(r):
+            wide = q_ref[r, :, ch * CWIDTH : (ch + 1) * CWIDTH].astype(F32)
+            rows = [wide[:, h * HD : (h + 1) * HD] for h in range(CHEADS * GQ)]
+            qs[r, ch * CROWS : (ch + 1) * CROWS] = jnp.concatenate(rows, axis=0).astype(BF16)
+
+    make_rows(0)
     pl.semaphore_wait(barrier, NG - 1 + NC - 1)
 
     def drain(ref, sem):
@@ -155,6 +122,8 @@
     own_n = pltpu.make_async_copy(new_ref.at[g], newv.at[g], loc_sem.at[NCH])
     own_p = pltpu.make_async_copy(plan_out.at[mz], plan_in.at[0], loc_sem.at[NCH + 1])
     for ch in range(NCH):
+        if ch > 0:
+            make_rows(ch)
         own_q[ch].start()
 
         @pl.loop(1, NG)
@@ -162,6 +131,40 @@
             gq_copy(ch, i).start()
 
         if ch == 0:
+            entry = lax.broadcasted_iota(I32, (1, 128), 1)
+            owner_row = jnp.full((1, 128), -1, I32)
+            page_row = jnp.zeros((1, 128), I32)
+            tok_row = jnp.zeros((1, 128), I32)
+            for r in range(REQ):
+                for s in range(SEL):
+                    at = entry == r * SEL + s
+                    owner_row = jnp.where(at, owner_ref[s, r], owner_row)
+                    page_row = jnp.where(at, page_ref[s, r], page_row)
+                    tok_row = jnp.where(at, jnp.clip(length_ref[r] - s * PAGE, 0, PAGE), tok_row)
+
+            shape = (NZ, 128)
+            lane = lax.broadcasted_iota(I32, shape, 1)
+            row = lax.broadcasted_iota(I32, shape, 0)
+            owners = jnp.broadcast_to(owner_row, shape)
+            pages = jnp.broadcast_to(page_row, shape)
+            tokens = jnp.broadcast_to(tok_row, shape)
+            plan = jnp.zeros(shape, I32)
+            for x in range(NX):
+                match = (owners == row + x * NZ) & (lane < NC)
+                first = jnp.min(jnp.where(match, lane, 999), axis=1, keepdims=True)
+                last = jnp.max(jnp.where(match, lane, -1), axis=1, keepdims=True)
+                is0 = lane == first
+                is1 = match & (lane == last) & (last > first)
+                for slot, here in enumerate((is0, is1)):
+                    for base, value in ((L_REQ, lane // SEL), (L_PAGE, pages), (L_TOK, tokens)):
+                        picked = jnp.sum(jnp.where(here, value, 0), axis=1, keepdims=True)
+                        plan = jnp.where(lane == x * 8 + base + slot, picked, plan)
+                    found = jnp.max(jnp.where(here, lane // SEL, -1), axis=1, keepdims=True)
+                    plan = jnp.where(lane == x * 8 + L_ID + slot, found, plan)
+            for z in range(NZ):
+                plan_out[z] = plan[z : z + 1]
+            own_plan = pltpu.make_async_copy(plan_out.at[mz], own_s, loc_sem.at[2 * NCH + 3])
+            own_plan.start()
             own_p.start()
 
             @pl.loop(1, NC)
@@ -273,35 +276,40 @@
 
     def attend(ch, k, dx):
         i = k * NX + dx
+        blank = jnp.zeros((GROUP, HD), BF16)
         for slot in range(CAP):
             page = plan_s[i, 0, mx * 8 + L_PAGE + slot]
             usable = token < plan_s[i, 0, mx * 8 + L_TOK + slot]
             query = recvq[ch, k, dx, slot]
-            scores = jnp.concatenate(
-                [
+            scores = []
+            for e in range(0, CHEADS, 2):
+                low, high = query[e * GROUP : (e + 1) * GROUP], query[(e + 1) * GROUP : (e + 2) * GROUP]
+                pair = jnp.concatenate(
+                    [jnp.concatenate([low, blank], axis=1), jnp.concatenate([blank, high], axis=1)], axis=0
+                )
+                at = ch * CHEADS + e
+                scores.append(
                     lax.dot_general(
-                        query[e * GROUP : (e + 1) * GROUP],
-                        kv_ref[page, :, (ch * CHEADS + e) * HD : (ch * CHEADS + e + 1) * HD],
+                        pair,
+                        kv_ref[page, :, at * HD : (at + 2) * HD],
                         (((1,), (1,)), ((), ())),
                         preferred_element_type=F32,
                     )
-                    for e in range(CHEADS)
-                ],
-                axis=0,
-            )
-            scores = jnp.where(usable, scores * SCALE, NEG)
+                )
+            scores = jnp.where(usable, jnp.concatenate(scores, axis=0) * SCALE, NEG)
             top = jnp.max(scores, axis=1, keepdims=True)
             weights = jnp.where(usable, jnp.exp(scores - top), 0.0)
             total = jnp.sum(weights, axis=1, keepdims=True)
             rounded = weights.astype(BF16)
-            for e in range(CHEADS):
+            for e in range(0, CHEADS, 2):
                 at = KVH + ch * CHEADS + e
                 mixed = jnp.dot(
-                    rounded[e * GROUP : (e + 1) * GROUP],
-                    kv_ref[page, :, at * HD : (at + 1) * HD],
+                    rounded[e * GROUP : (e + 2) * GROUP],
+                    kv_ref[page, :, at * HD : (at + 2) * HD],
                     preferred_element_type=F32,
-                )
-                outb[ch, k, dx, slot, e * GROUP : (e + 1) * GROUP] = mixed.astype(BF16)
+                ).astype(BF16)
+                outb[ch, k, dx, slot, e * GROUP : (e + 1) * GROUP] = mixed[:GROUP, :HD]
+                outb[ch, k, dx, slot, (e + 1) * GROUP : (e + 2) * GROUP] = mixed[GROUP:, HD:]
             stato[ch, k, dx, slot : slot + 1] = rows_to_lanes(top, eye)
             stato[ch, k, dx, CAP + slot : CAP + slot + 1] = rows_to_lanes(total, eye)
 
@@ -391,9 +399,10 @@
             ),
         ]
 
-    def link(ch, k):
-        x_done(ch, k)
-        for half in range(2):
+    def link(ch, *order):
+        for k in dict.fromkeys(k for k, _ in order):
+            x_done(ch, k)
+        for k, half in order:
             if k == 3 and half == 0 or k == 5 and half == 1:
                 outer = 4
             elif k in (1, 2):
@@ -419,12 +428,10 @@
             for copy in c_copies(ch, k, half):
                 copy.start()
 
-    def f_copy(ch, i):
+    def f_copy(ch, to):
         part = pl.ds(ch * CWIDTH, CWIDTH)
-        src, dst = (g + i) % NG, g
-        return pltpu.make_async_remote_copy(
-            fin.at[ch, src], out_ref.at[dst, :, part], f_send, f_recv,
-            device_id={"grp": (g + i) % NG},
+        return pltpu.make_async_remote_copy(
+            fin.at[ch, to], out_ref.at[g, :, part], f_send, f_recv, device_id={"grp": to}
         )
 
     own_f = [
@@ -434,27 +441,28 @@
 
     def finish(ch):
         x_done(ch, 0)
-        for outer, half in ((1, 0), (1, 1), (7, 0), (7, 1)):
-            for copy in c_copies(ch, outer, half):
-                copy.wait_recv()
-
-        @pl.loop(1, NG + 1)
-        def _(i):
-            r = (g + i) % NG
-            half, rr = r // HALF, r % HALF
-            parts = x_parts(ch, 0, r) + [brought(ch, 0, half, rr), brought(ch, NZ, half, rr)]
-            new = (newmix[ch, r], newtop[ch, pl.ds(r, 1), :], newsum[ch, pl.ds(r, 1), :])
-            result, _, _ = merge(parts, new)
-            pieces = [result[h * STEPS : (h + 1) * STEPS] for h in range(CHEADS * GQ)]
-            fin[ch, r] = jnp.concatenate(pieces, axis=1).astype(BF16)
-
-            @pl.when(i < NG)
-            def _():
-                f_copy(ch, i).start()
-
-            @pl.when(i == NG)
-            def _():
-                own_f[ch].start()
+        for half in range(2):
+            for outer in (1, 7):
+                for copy in c_copies(ch, outer, half):
+                    copy.wait_recv()
+
+            @pl.loop(0, HALF)
+            def _(t):
+                rr = (g + 1 + t) % HALF
+                r = half * HALF + rr
+                parts = x_parts(ch, 0, r) + [brought(ch, 0, half, rr), brought(ch, NZ, half, rr)]
+                new = (newmix[ch, r], newtop[ch, pl.ds(r, 1), :], newsum[ch, pl.ds(r, 1), :])
+                result, _, _ = merge(parts, new)
+                pieces = [result[h * STEPS : (h + 1) * STEPS] for h in range(CHEADS * GQ)]
+                fin[ch, r] = jnp.concatenate(pieces, axis=1).astype(BF16)
+
+                @pl.when(r != g)
+                def _():
+                    f_copy(ch, r).start()
+
+                @pl.when(r == g)
+                def _():
+                    own_f[ch].start()
 
     steps = [(0,), (1, 7), (2, 6), (3, 5), (4,)]
 
@@ -492,44 +500,38 @@
     forward(0, 3, [(0, 1), (0, 7)])
     forward(0, 4, [(0, 2), (0, 6)])
     forward(1, 1, [(0, 3), (0, 5)])
+    give(0, 3)
     forward(1, 2, [(0, 4)])
     give(0, 4)
-    give(0, 3)
     give(0, 5)
     forward(1, 3, [(1, 1), (1, 7)])
-    new_tokens(0)
-    link(0, 4)
+    link(0, (4, 0), (4, 1))
     forward(1, 4, [(1, 2), (1, 6)])
     give(0, 2)
     give(0, 6)
-    link(0, 3)
-    link(0, 5)
+    link(0, (3, 1), (5, 0), (3, 0), (5, 1))
     work(1, 3)
     work(1, 5)
     give(0, 1)
     give(0, 7)
-    link(0, 2)
-    link(0, 6)
     work(1, 4)
     give(1, 4)
+    link(0, (2, 1), (6, 0), (2, 0), (6, 1))
     give(1, 3)
     give(1, 5)
-    link(0, 1)
-    link(0, 7)
-    link(1, 4)
+    link(1, (4, 0), (4, 1))
+    link(0, (1, 1), (7, 0), (1, 0), (7, 1))
     give(1, 2)
     give(1, 6)
-    new_tokens(1)
-    link(1, 3)
-    link(1, 5)
+    link(1, (3, 1), (5, 0), (3, 0), (5, 1))
     give(1, 1)
     give(1, 7)
+    new_tokens(0)
+    finish(0)
+    link(1, (2, 1), (6, 0), (2, 0), (6, 1))
     give(1, 0)
-    finish(0)
-    link(1, 2)
-    link(1, 6)
-    link(1, 1)
-    link(1, 7)
+    new_tokens(1)
+    link(1, (1, 1), (7, 0), (1, 0), (7, 1))
     finish(1)
 
     for ch in range(NCH):

time: 137 us -> 133 us (0.971)
  Pallas kernels: 135 us -> 131 us
    pallas_call x1, Pallas kernels: 135 us -> 131 us  [per_device(): pl.pallas_call(kernel, out_shape=jax.ShapeDtypeStruct((REQ, STEPS, KVH *...]
where the time goes in v4:
time: 133 us
  Pallas kernels  131 us (98%)
  local copies, waits for them, and re-layouts  2.02 us (2%)
    pallas_call x1, Pallas kernels, per_device(): pl.pallas_call(kernel, out_shape=jax.ShapeDtypeStruct((REQ, STEPS, KVH *...  131 us

profile of v4, /device:TPU:1, one launch (start us, length us, event | category | flops | bytes accessed | tf_op | source)
XLA Modules:
  0.0 133.2 jit_solution(6578921065673271940)
XLA Ops:
  0.0 131.2 %paged_decode.1 = bf16[8,4,8192]{2,1,0:T(4,128)(2,1)} custom-call(bf16[8,4,8192]{2,1,0:T(4,128)(2,1)} %q_ref.1, bf16[8,4,2048]{2,1,0:T(4,128)(2,1)} %new_ref.1, s32[4,8]{1,0:T(4,128)} %bitcast.4, s32[4,8]{1,0:T(4,128)} %bitcast.5, s32[8]{0:T(128)} %length_ref.1, bf16[16,128,2048]{2,1,0:T(8,128)(2,1)} %kv_hbm.1), custom_call_target="tpu_custom_call" | custom-call | tf_op jit(solution)/shard_map/paged_decode/pallas_call | solution.py:558
  131.2 2.0 %copy.8 = bf16[8,4,8192]{2,1,0:T(4,128)(2,1)} copy(bf16[8,4,8192]{2,1,0:T(4,128)(2,1)} %paged_decode.1) | data formatting | bytes 1048576

commit v5 on v4

--- a/solution.py
+++ b/solution.py
@@ -44,7 +44,7 @@
     return jnp.sum(jnp.where(eye, jnp.broadcast_to(line, (CROWS, 128)), 0.0), axis=1, keepdims=True)
 
 
-def kernel(q_ref, new_ref, owner_ref, page_ref, length_ref, kv_hbm, out_ref, kv_ref, *rest):
+def kernel(q_hbm, new_ref, owner_ref, page_ref, length_ref, kv_hbm, out_ref, kv_ref, *rest):
     rest = list(rest)
 
     def take(count):
@@ -57,7 +57,7 @@
 
     ag, xret, xstat, dense, dstat = (take_each(NZ) for _ in range(5))
     chain, cstat = (take_each(NZ + 1) for _ in range(2))
-    qs, newv, xsend, recvq, outb, stato, plan_out, plan_in, plan_s, own_s, newmix, newtop, newsum, fin = take(14)
+    q_ref, qs, newv, xsend, recvq, outb, stato, plan_out, plan_in, plan_s, own_s, newmix, newtop, newsum, fin = take(15)
     kv_sem, loc_sem, gq_send, gq_recv, gn_send, gn_recv, pl_send, pl_recv = take(8)
     ag_send, ag_recv, x_send, x_recv, o_send, o_recv, s_send, s_recv = take(8)
     c_send, c_recv, cs_send, cs_recv, f_send, f_recv = take(6)
@@ -68,6 +68,9 @@
 
     def node(x, z):
         return {"cache": (x % NX) * NZ + z % NZ}
+
+    q_copy = pltpu.make_async_copy(q_hbm, q_ref, loc_sem.at[2 * NCH + 4])
+    q_copy.start()
 
     barrier = pltpu.get_barrier_semaphore()
 
@@ -89,6 +92,7 @@
             rows = [wide[:, h * HD : (h + 1) * HD] for h in range(CHEADS * GQ)]
             qs[r, ch * CROWS : (ch + 1) * CROWS] = jnp.concatenate(rows, axis=0).astype(BF16)
 
+    q_copy.wait()
     make_rows(0)
     pl.semaphore_wait(barrier, NG - 1 + NC - 1)
 
@@ -415,7 +419,7 @@
                 for copy in c_copies(ch, outer, half):
                     copy.wait_recv()
 
-            @pl.loop(0, HALF)
+            @pl.loop(0, HALF, unroll=4)
             def _(rr):
                 parts = x_parts(ch, k, half * HALF + rr)
                 if outer is not None:
@@ -446,7 +450,7 @@
                 for copy in c_copies(ch, outer, half):
                     copy.wait_recv()
 
-            @pl.loop(0, HALF)
+            @pl.loop(0, HALF, unroll=4)
             def _(t):
                 rr = (g + 1 + t) % HALF
                 r = half * HALF + rr
@@ -508,14 +512,14 @@
     link(0, (4, 0), (4, 1))
     forward(1, 4, [(1, 2), (1, 6)])
     give(0, 2)
+    link(0, (3, 1), (5, 0), (3, 0), (5, 1))
     give(0, 6)
-    link(0, (3, 1), (5, 0), (3, 0), (5, 1))
     work(1, 3)
     work(1, 5)
+    work(1, 4)
+    give(1, 4)
     give(0, 1)
     give(0, 7)
-    work(1, 4)
-    give(1, 4)
     link(0, (2, 1), (6, 0), (2, 0), (6, 1))
     give(1, 3)
     give(1, 5)
@@ -551,14 +555,13 @@
 
 def per_device(queries, new_kv, kv_cache, page_owner, page_index, lengths):
     dma = pltpu.SemaphoreType.DMA
-    vmem = pl.BlockSpec(memory_space=pltpu.VMEM)
     smem = pl.BlockSpec(memory_space=pltpu.SMEM)
     hbm = pl.BlockSpec(memory_space=pl.ANY)
     block = pltpu.VMEM((REQ, CROWS, HD), BF16)
     return pl.pallas_call(
         kernel,
         out_shape=jax.ShapeDtypeStruct((REQ, STEPS, KVH * GQ * HD), BF16),
-        in_specs=[vmem, vmem, smem, smem, smem, hbm],
+        in_specs=[hbm, hbm, smem, smem, smem, hbm],
         out_specs=hbm,
         scratch_shapes=[
             pltpu.VMEM((PAGES, PAGE, 2 * KVH * HD), BF16),
@@ -569,6 +572,7 @@
             *[pltpu.VMEM((2, 8, 128), F32)] * (NCH * NZ),
             *[block] * (NCH * (NZ + 1)),
             *[pltpu.VMEM((2, 8, 128), F32)] * (NCH * (NZ + 1)),
+            pltpu.VMEM((REQ, STEPS, KVH * GQ * HD), BF16),
             pltpu.VMEM((REQ, ROWS, HD), BF16),
             pltpu.VMEM((REQ, STEPS, 2 * KVH * HD), BF16),
             pltpu.VMEM((NCH, NZ, NX - 1, CAP, CROWS, HD), BF16),
@@ -584,7 +588,7 @@
             pltpu.VMEM((NCH, REQ, 128), F32),
             pltpu.VMEM((NCH, REQ, STEPS, CWIDTH), BF16),
             dma,
-            dma((2 * NCH + 4,)),
+            dma((2 * NCH + 5,)),
             dma,
             dma((NCH,)),
             *[dma] * 4,

time: 133 us -> 130 us (0.977)
  Pallas kernels: 131 us -> 128 us
    pallas_call x1, Pallas kernels: 131 us -> 128 us  [per_device(): pl.pallas_call(kernel, out_shape=jax.ShapeDtypeStruct((REQ, STEPS, KVH *...]
where the time goes in v5:
time: 130 us
  Pallas kernels  128 us (98%)
  local copies, waits for them, and re-layouts  2.02 us (2%)
    pallas_call x1, Pallas kernels, per_device(): pl.pallas_call(kernel, out_shape=jax.ShapeDtypeStruct((REQ, STEPS, KVH *...  128 us

profile of v5, /device:TPU:1, one launch (start us, length us, event | category | flops | bytes accessed | tf_op | source)
XLA Modules:
  0.0 129.5 jit_solution(15598856699764331060)
XLA Ops:
  0.0 127.5 %paged_decode.1 = bf16[8,4,8192]{2,1,0:T(4,128)(2,1)} custom-call(bf16[8,4,8192]{2,1,0:T(4,128)(2,1)} %q_hbm.1, bf16[8,4,2048]{2,1,0:T(4,128)(2,1)} %new_ref.1, s32[4,8]{1,0:T(4,128)} %bitcast.4, s32[4,8]{1,0:T(4,128)} %bitcast.5, s32[8]{0:T(128)} %length_ref.1, bf16[16,128,2048]{2,1,0:T(8,128)(2,1)} %kv_hbm.1), custom_call_target="tpu_custom_call" | custom-call | tf_op jit(solution)/shard_map/paged_decode/pallas_call | solution.py:561
  127.5 2.0 %copy.8 = bf16[8,4,8192]{2,1,0:T(4,128)(2,1)} copy(bf16[8,4,8192]{2,1,0:T(4,128)(2,1)} %paged_decode.1) | data formatting | bytes 1048576

commit v6 on v5

--- a/solution.py
+++ b/solution.py
@@ -514,12 +514,14 @@
     give(0, 2)
     link(0, (3, 1), (5, 0), (3, 0), (5, 1))
     give(0, 6)
+    new_tokens(0)
     work(1, 3)
     work(1, 5)
     work(1, 4)
     give(1, 4)
     give(0, 1)
     give(0, 7)
+    new_tokens(1)
     link(0, (2, 1), (6, 0), (2, 0), (6, 1))
     give(1, 3)
     give(1, 5)
@@ -530,11 +532,9 @@
     link(1, (3, 1), (5, 0), (3, 0), (5, 1))
     give(1, 1)
     give(1, 7)
-    new_tokens(0)
     finish(0)
     link(1, (2, 1), (6, 0), (2, 0), (6, 1))
     give(1, 0)
-    new_tokens(1)
     link(1, (1, 1), (7, 0), (1, 0), (7, 1))
     finish(1)
 

time: 130 us -> 134 us (1.031); the launches traced: 130 us -> 132 us
  Pallas kernels: 128 us -> 130 us
    pallas_call x1, Pallas kernels: 128 us -> 130 us  [per_device(): pl.pallas_call(kernel, out_shape=jax.ShapeDtypeStruct((REQ, STEPS, KVH *...]
where the time goes in v6:
time: 134 us; the launch traced here: 132 us
  Pallas kernels  130 us (97%)
  local copies, waits for them, and re-layouts  2.02 us (2%)
    pallas_call x1, Pallas kernels, per_device(): pl.pallas_call(kernel, out_shape=jax.ShapeDtypeStruct((REQ, STEPS, KVH *...  130 us

profile of v6, /device:TPU:1, one launch (start us, length us, event | category | flops | bytes accessed | tf_op | source)
XLA Modules:
  0.0 132.1 jit_solution(2815050088220856856)
XLA Ops:
  0.0 130.1 %paged_decode.1 = bf16[8,4,8192]{2,1,0:T(4,128)(2,1)} custom-call(bf16[8,4,8192]{2,1,0:T(4,128)(2,1)} %q_hbm.1, bf16[8,4,2048]{2,1,0:T(4,128)(2,1)} %new_ref.1, s32[4,8]{1,0:T(4,128)} %bitcast.4, s32[4,8]{1,0:T(4,128)} %bitcast.5, s32[8]{0:T(128)} %length_ref.1, bf16[16,128,2048]{2,1,0:T(8,128)(2,1)} %kv_hbm.1), custom_call_target="tpu_custom_call" | custom-call | tf_op jit(solution)/shard_map/paged_decode/pallas_call | solution.py:561
  130.1 2.0 %copy.8 = bf16[8,4,8192]{2,1,0:T(4,128)(2,1)} copy(bf16[8,4,8192]{2,1,0:T(4,128)(2,1)} %paged_decode.1) | data formatting | bytes 1048576
